TPU v7x, 32 devices: a whole 2x2x4 slice. The times are simulated.
32 devices in a mesh: dp: 8 (over y, x, core), mp: 4 (over z).
Axes of the slice: x: 2, y: 2, z: 4, core: 2. Of those that a mesh axis runs over, the one named last changes fastest.
Arguments:
- tokens: bfloat16 [32768, 512], P(('dp', 'mp')), may hold values from -6 to 6
- cotangent: bfloat16 [32768, 512], P(('dp', 'mp')), may hold values from -13.5 to 13.5
- master: float32 [4, 64, 128, 128], P('mp', 'dp'), may hold values from -0.2165625 to 0.2165625
- moment_one: float32 [4, 64, 128, 128], P('mp', 'dp'), may hold values from -615.46574 to 615.46574
- moment_two: float32 [4, 64, 128, 128], P('mp', 'dp'), may hold values from 838.8608 to 94699.52
- basis_left: float32 [4, 64, 128, 128], P('mp', 'dp'), may hold values from -1 to 1, as said below
- basis_right: float32 [4, 64, 128, 128], P('mp', 'dp'), may hold values from -1 to 1, as said below
- owner: int32 [64], replicated, may hold values from 0 to 7, as said below
- gains: float32 [2, 512], replicated, may hold values from 0.5 to 1.5
- gain_moment_one: float32 [2, 512], replicated, may hold values from -470.65027 to 470.65027
- gain_moment_two: float32 [2, 512], replicated, may hold values from 13844.48 to 55377.92
Outputs:
- block_out: bfloat16 [32768, 512], P(('dp', 'mp'))
- input_grad: float32 [32768, 512], P(('dp', 'mp'))
- moment_one_new: float32 [4, 64, 128, 128], P('mp', 'dp')
- moment_two_new: float32 [4, 64, 128, 128], P('mp', 'dp')
- master_new: float32 [4, 64, 128, 128], P('mp', 'dp')
- master_low: bfloat16 [4, 64, 128, 128], P('mp', 'dp')
- gain_moment_one_new: float32 [2, 512], replicated
- gain_moment_two_new: float32 [2, 512], replicated
- gains_new: float32 [2, 512], replicated
- forget_mean: float32 [], replicated
Inputs may be any that keep to these rules, and one draw needn't show every extreme that they name: `owner`: every index of dp appears exactly 64 * 4 / 32 times. `basis_left`: every [128, 128] block is an orthogonal matrix. `basis_right`: every [128, 128] block is an orthogonal matrix.
All inputs are finite; a program needn't handle non-finite values.
Results may differ from a plain program's by a relative error of at most 0.0079.
Values may be sent and summed in bfloat16 or wider, within the bound.
A program may use at most 192 MiB of HBM per device.

v0:
```python
import jax
import jax.numpy as jnp
from jax import lax
from jax.sharding import PartitionSpec as P

D = 512
H = 1024
FF = 2048
BLK = 128
STEP = 10
L = 1024


norm_eps = 1e-05
beta_one = 0.5
beta_two = 0.5
adam_eps = 1e-08
learn_rate = 0.02
gain_rate = 0.1
weight_decay = 0.1
highest = lax.Precision.HIGHEST


def rms_norm(values, gain):
    return values * lax.rsqrt(jnp.mean(values * values, axis=-1, keepdims=True) + norm_eps) * gain


def gate_terms(pre):
    forget = jax.nn.sigmoid(pre[:, 0])
    admit = jax.nn.sigmoid(pre[:, 1])
    total = forget + admit
    return (forget / total, admit / total * pre[:, 2])


def combine_steps(earlier, later):
    return (earlier[0] * later[0], later[0] * earlier[1] + later[1])


def exact_gelu(values):
    return jax.nn.gelu(values, approximate=False)


def assemble(weight_stack, shard_h, shard_f):
    parts = weight_stack.shape[0]
    row_tiles = D // BLK
    col_tiles = (3 * shard_h + shard_f) // BLK
    low_tiles = (shard_h + shard_f) // BLK
    upper = weight_stack[:, : row_tiles * col_tiles].reshape(parts, row_tiles, col_tiles, BLK, BLK)
    upper = upper.transpose(0, 1, 3, 2, 4).reshape(parts, D, col_tiles * BLK)
    lower = weight_stack[:, row_tiles * col_tiles :].reshape(parts, low_tiles, row_tiles, BLK, BLK)
    lower = lower.transpose(0, 1, 3, 2, 4).reshape(parts, low_tiles * BLK, D)
    w_gate = (
        upper[:, :, : 3 * shard_h]
        .reshape(parts, D, 3, shard_h)
        .transpose(1, 2, 0, 3)
        .reshape(D, 3 * parts * shard_h)
    )
    w_up = upper[:, :, 3 * shard_h :].transpose(1, 0, 2).reshape(D, parts * shard_f)
    w_out = lower[:, :shard_h].reshape(parts * shard_h, D)
    w_down = lower[:, shard_h:].reshape(parts * shard_f, D)
    return (w_gate, w_up, w_out, w_down)


def disassemble(grad_gate, grad_up, grad_out, grad_down, parts, shard_h, shard_f):
    row_tiles = D // BLK
    col_tiles = (3 * shard_h + shard_f) // BLK
    low_tiles = (shard_h + shard_f) // BLK
    gate_part = (
        grad_gate.reshape(D, 3, parts, shard_h).transpose(2, 0, 1, 3).reshape(parts, D, 3 * shard_h)
    )
    up_part = grad_up.reshape(D, parts, shard_f).transpose(1, 0, 2)
    upper = jnp.concatenate([gate_part, up_part], axis=2)
    upper = upper.reshape(parts, row_tiles, BLK, col_tiles, BLK).transpose(0, 1, 3, 2, 4)
    upper = upper.reshape(parts, row_tiles * col_tiles, BLK, BLK)
    lower = jnp.concatenate(
        [grad_out.reshape(parts, shard_h, D), grad_down.reshape(parts, shard_f, D)], axis=1
    )
    lower = lower.reshape(parts, low_tiles, BLK, row_tiles, BLK).transpose(0, 1, 3, 2, 4)
    lower = lower.reshape(parts, low_tiles * row_tiles, BLK, BLK)
    return jnp.concatenate([upper, lower], axis=1)


def adam_update(first_old, second_old, gradient):
    first_new = beta_one * first_old + (1.0 - beta_one) * gradient
    second_new = beta_two * second_old + (1.0 - beta_two) * gradient * gradient
    first_hat = first_new / (1.0 - beta_one**STEP)
    second_hat = second_new / (1.0 - beta_two**STEP)
    return (first_new, second_new, first_hat / (jnp.sqrt(second_hat) + adam_eps))


def soap_update(master, moment_one, moment_two, basis_left, basis_right, grads):
    left_side = jnp.einsum("pkab,pkac->pkbc", basis_left, grads, precision=highest)
    rotated = jnp.einsum("pkbc,pkcd->pkbd", left_side, basis_right, precision=highest)
    first_new, second_new, direction = adam_update(moment_one, moment_two, rotated)
    turned = jnp.einsum("pkab,pkbc->pkac", basis_left, direction, precision=highest)
    turned = jnp.einsum("pkac,pkdc->pkad", turned, basis_right, precision=highest)
    master_new = master - learn_rate * (turned + weight_decay * master)
    return (first_new, second_new, master_new)


def project_rows(normed, weight):
    return jnp.dot(
        lax.all_gather(normed, "mp", axis=0, tiled=True), weight, preferred_element_type=jnp.float32
    )


def reduce_rows(activation, weight):
    return lax.psum_scatter(
        jnp.dot(activation, weight, preferred_element_type=jnp.float32),
        "mp",
        scatter_dimension=0,
        tiled=True,
    )


def spread_grads(grad_low, activation, weight):
    shard_rows = lax.all_gather(grad_low, "mp", axis=0, tiled=True)
    back_rows = lax.dot_general(
        shard_rows, weight, (((1,), (1,)), ((), ())), preferred_element_type=jnp.float32
    )
    weight_part = lax.dot_general(
        activation, shard_rows, (((0,), (0,)), ((), ())), preferred_element_type=jnp.float32
    )
    return (back_rows, weight_part)


def collect_rows(grad_low, weight):
    return lax.psum_scatter(
        lax.dot_general(
            grad_low, weight, (((1,), (1,)), ((), ())), preferred_element_type=jnp.float32
        ),
        "mp",
        scatter_dimension=0,
        tiled=True,
    )


def weight_grad(normed, grad_low):
    return lax.dot_general(
        lax.all_gather(normed, "mp", axis=0, tiled=True),
        grad_low,
        (((0,), (0,)), ((), ())),
        preferred_element_type=jnp.float32,
    )


def on_device(
    tokens,
    cotangent,
    master,
    moment_one,
    moment_two,
    basis_left,
    basis_right,
    owner,
    gains,
    gain_moment_one,
    gain_moment_two,
):
    model_parts = lax.axis_size("mp")
    data_parts = lax.axis_size("dp")
    shard_h = H // model_parts
    shard_f = FF // model_parts
    row_count = tokens.shape[0]
    token_total = row_count * data_parts * model_parts
    slot_order = jnp.argsort(owner, stable=True)
    block_rank = jnp.argsort(slot_order, stable=True)
    stored = lax.all_gather(master.astype(jnp.bfloat16), "dp", axis=1, tiled=True)
    weight_stack = stored[:, block_rank]
    w_gate, w_up, w_out, w_down = assemble(weight_stack, shard_h, shard_f)
    tokens_wide = tokens.astype(jnp.float32)
    normed_one = rms_norm(tokens_wide, gains[0]).astype(jnp.bfloat16)
    pre = project_rows(normed_one, w_gate)
    rows_all = pre.shape[0]
    seq_count = rows_all // L
    pre_split = pre.reshape(rows_all, 3, shard_h)
    keep_rate, write_term = gate_terms(pre_split)
    keep_seq = keep_rate.reshape(seq_count, L, shard_h)
    _, state = lax.associative_scan(
        combine_steps, (keep_seq, write_term.reshape(seq_count, L, shard_h)), axis=1
    )
    state_low = state.reshape(rows_all, shard_h).astype(jnp.bfloat16)
    first_row = lax.axis_index("dp") * rows_all
    place = first_row.astype(jnp.float32) + jnp.arange(rows_all, dtype=jnp.float32) + 1.0
    forget_part = jnp.sum(keep_rate * (place / float(token_total))[:, None])
    forget_total = lax.psum(forget_part, ("dp", "mp"))
    mixed = tokens_wide + reduce_rows(state_low, w_out)
    normed_two = rms_norm(mixed, gains[1]).astype(jnp.bfloat16)
    upward = project_rows(normed_two, w_up)
    act_low = exact_gelu(upward).astype(jnp.bfloat16)
    block_out = (mixed + reduce_rows(act_low, w_down)).astype(jnp.bfloat16)
    d_act, grad_down = spread_grads(cotangent, act_low, w_down)
    _, gelu_pull = jax.vjp(exact_gelu, upward)
    d_up = gelu_pull(d_act)[0].astype(jnp.bfloat16)
    d_normed_two = collect_rows(d_up, w_up)
    grad_up = weight_grad(normed_two, d_up)
    _, norm_two_pull = jax.vjp(rms_norm, mixed, gains[1])
    mixed_back, grad_gain_two = norm_two_pull(d_normed_two)
    d_mixed = cotangent.astype(jnp.float32) + mixed_back
    d_mixed_low = d_mixed.astype(jnp.bfloat16)
    d_state, grad_out = spread_grads(d_mixed_low, state_low, w_out)
    keep_next = jnp.concatenate(
        [keep_seq[:, 1:], jnp.zeros((seq_count, 1, shard_h), jnp.float32)], axis=1
    )
    _, carried = lax.associative_scan(
        combine_steps, (keep_next, d_state.reshape(seq_count, L, shard_h)), reverse=True, axis=1
    )
    state_prev = jnp.concatenate(
        [jnp.zeros((seq_count, 1, shard_h), jnp.float32), state[:, :-1]], axis=1
    )
    d_keep = (carried * state_prev).reshape(rows_all, shard_h)
    d_write = carried.reshape(rows_all, shard_h)
    _, gate_pull = jax.vjp(gate_terms, pre_split)
    d_pre = gate_pull((d_keep, d_write))[0].reshape(rows_all, 3 * shard_h).astype(jnp.bfloat16)
    d_normed_one = collect_rows(d_pre, w_gate)
    grad_gate = weight_grad(normed_one, d_pre)
    _, norm_one_pull = jax.vjp(rms_norm, tokens_wide, gains[0])
    tokens_back, grad_gain_one = norm_one_pull(d_normed_one)
    input_grad = d_mixed + tokens_back
    gain_local = jnp.stack([grad_gain_one, grad_gain_two])
    gain_grad = lax.psum(gain_local, ("dp", "mp"))
    natural = disassemble(
        grad_gate, grad_up, grad_out, grad_down, weight_stack.shape[0], shard_h, shard_f
    )
    owned = lax.psum_scatter(natural[:, slot_order], "dp", scatter_dimension=1, tiled=True)
    first_new, second_new, master_new = soap_update(
        master, moment_one, moment_two, basis_left, basis_right, owned
    )
    gain_first, gain_second, gain_direction = adam_update(
        gain_moment_one, gain_moment_two, gain_grad
    )
    gains_new = gains - gain_rate * gain_direction
    forget_mean = forget_total / (H * (token_total + 1) / 2.0)
    return (
        block_out,
        input_grad,
        first_new,
        second_new,
        master_new,
        master_new.astype(jnp.bfloat16),
        gain_first,
        gain_second,
        gains_new,
        forget_mean,
    )


def solution(mesh):
    placed = (
        P(("dp", "mp"), None),
        P(("dp", "mp"), None),
        P("mp", "dp", None, None),
        P("mp", "dp", None, None),
        P("mp", "dp", None, None),
        P("mp", "dp", None, None),
        P("mp", "dp", None, None),
        P(),
        P(),
        P(),
        P(),
    )
    return jax.shard_map(
        on_device,
        mesh=mesh,
        in_specs=placed,
        out_specs=(
            P(("dp", "mp"), None),
            P(("dp", "mp"), None),
            P("mp", "dp", None, None),
            P("mp", "dp", None, None),
            P("mp", "dp", None, None),
            P("mp", "dp", None, None),
            P(),
            P(),
            P(),
            P(),
        ),
        check_vma=False,
    )
```

profile of v0, /device:TPU:0, one launch (start us, length us, event | category | flops | bytes accessed | tf_op | source)
XLA Modules:
  0.0 1607.7 jit_solution(6219907944056662205)
XLA Ops:
  18.2 23.0 %all-gather.8.cloned.1.call-done = bf16[1,64,128,128]{3,2,0,1:T(8,128)(2,1)} async-done(((bf16[1,8,128,128]{3,2,0,1:T(8,128)(2,1)}), bf16[1,64,128,128]{3,2,0,1:T(8,128)(2,1)}) %all-gather.8.cloned.1.call-update) | async-done | bytes 2097168 | tf_op jit(solution)/shard_map/all_gather | solution.py:168
  52.1 72.0 %all-gather.6.cloned.1.call-done = bf16[4096,512]{1,0:T(8,128)(2,1)} async-done(((bf16[1024,512]{1,0:T(8,128)(2,1)}), bf16[4096,512]{1,0:T(8,128)(2,1)}) %all-gather.6.cloned.1.call-update) | async-done | bytes 4194320 | tf_op jit(solution)/shard_map/all_gather | solution.py:103
  124.1 5.3 fusion.26
  138.4 11.7 slice.537
  150.2 11.8 slice.533
  161.9 11.9 slice.532
  174.6 11.9 slice.605
  186.5 11.8 slice.535
  198.2 11.8 slice.534
  210.0 5.3 fusion.102
  215.3 7.3 slice.543
  222.7 7.3 slice.539
  230.0 7.4 slice.538
  275.3 5.0 pad.150
  286.7 9.4 pad.151
  296.1 6.1 pad.152
  306.3 4.5 fusion.72
  310.8 143.1 %reduce-scatter.6.cloned.1.call-done = f32[1024,512]{1,0:T(8,128)} async-done(((f32[4096,512]{1,0:T(8,128)}), f32[1024,512]{1,0:T(8,128)}) %reduce-scatter.6.cloned.1.call-update) | async-done | bytes 2097168 | tf_op jit(solution)/shard_map/reduce_scatter | solution.py:108
  458.0 81.0 %all-gather.10.cloned.1.call-done = bf16[4096,512]{1,0:T(8,128)(2,1)} async-done(((bf16[1024,512]{1,0:T(8,128)(2,1)}), bf16[4096,512]{1,0:T(8,128)(2,1)}) %all-gather.10.cloned.1.call-update) | async-done | bytes 4194320 | tf_op jit(solution)/shard_map/all_gather | solution.py:103
  539.0 23.3 %multiply_convert_fusion = (bf16[4096,512]{1,0:T(8,128)(2,1)}, f32[4096,512]{1,0:T(8,128)}, f32[4096,512]{1,0:T(8,128)}) fusion(bf16[4096,512]{1,0:T(8,128)(2,1)} %all-gather.10.cloned.1.call-done, bf16[1,512,1280]{1,2,0:T(8,128)(2,1)} %reshape.175), kind=kOutput, calls=%fused_computation.14 | convolution fusion | flops 2283798528 | bytes 25690112 | tf_op jit(solution)/shard_map/dot_general | solution.py:102
  562.3 57.5 %all-gather.12.cloned.1.call-done = bf16[4096,512]{1,0:T(8,128)(2,1)} async-done(((bf16[1024,512]{1,0:T(8,128)(2,1)}), bf16[4096,512]{1,0:T(8,128)(2,1)}) %all-gather.12.cloned.1.call-update) | async-done | bytes 4194320 | tf_op jit(solution)/shard_map/all_gather | solution.py:117
  619.8 9.2 fusion.6
  631.0 5.6 fusion.65
  636.6 143.1 %reduce-scatter.10.cloned.1.call-done = f32[1024,512]{1,0:T(8,128)} async-done(((f32[4096,512]{1,0:T(8,128)}), f32[1024,512]{1,0:T(8,128)}) %reduce-scatter.10.cloned.1.call-update) | async-done | bytes 2097168 | tf_op jit(solution)/shard_map/reduce_scatter | solution.py:128
  789.8 12.0 slice.622
  801.9 11.8 slice.615
  813.6 11.8 slice.613
  825.4 16.6 %slice.623 = f32[4,512,256]{2,1,0:T(8,128)} reverse(f32[4,512,256]{2,1,0:T(8,128)} %slice.622), dimensions={1} | reverse | bytes 4194304 | tf_op jit(solution)/shard_map/slice | solution.py:205
  842.0 17.2 %slice.614 = f32[4,511,256]{2,1,0:T(8,128)} reverse(f32[4,511,256]{2,1,0:T(8,128)} %slice.613), dimensions={1} | reverse | bytes 4186112 | tf_op jit(solution)/shard_map/slice | solution.py:205
  859.2 16.6 %slice.616 = f32[4,512,256]{2,1,0:T(8,128)} reverse(f32[4,512,256]{2,1,0:T(8,128)} %slice.615), dimensions={1} | reverse | bytes 4194304 | tf_op jit(solution)/shard_map/slice | solution.py:205
  875.8 6.3 slice_add_fusion
  895.8 11.8 slice.691
  907.6 11.8 slice.619
  919.4 11.7 slice.617
  931.1 16.6 %slice.618 = f32[4,512,256]{2,1,0:T(8,128)} reverse(f32[4,512,256]{2,1,0:T(8,128)} %slice.617), dimensions={1} | reverse | bytes 4194304 | tf_op jit(solution)/shard_map/slice | solution.py:205
  947.7 16.6 %slice.620 = f32[4,512,256]{2,1,0:T(8,128)} reverse(f32[4,512,256]{2,1,0:T(8,128)} %slice.619), dimensions={1} | reverse | bytes 4194304 | tf_op jit(solution)/shard_map/slice | solution.py:205
  964.4 6.1 fusion.101
  970.5 7.3 slice.629
  977.8 7.3 slice.625
  985.1 7.4 slice.624
  993.9 7.4 slice.689
  1001.3 7.3 slice.627
  1008.5 7.3 slice.626
  1072.1 17.2 %slice.692 = f32[4,511,256]{2,1,0:T(8,128)} reverse(f32[4,511,256]{2,1,0:T(8,128)} %slice.691), dimensions={1} | reverse | bytes 4186112 | tf_op jit(solution)/shard_map/slice | solution.py:205
  1117.2 5.0 pad.169
  1122.1 5.1 pad.170
  1135.8 9.4 pad.171
  1145.2 9.3 pad.172
  1154.5 6.0 add.475
  1160.5 32.5 %rev.2 = f32[4,1024,256]{2,1,0:T(8,128)} reverse(f32[4,1024,256]{2,1,0:T(8,128)} %add.475), dimensions={1} | reverse | bytes 8388608 | tf_op jit(solution)/shard_map/rev | solution.py:205
  1197.6 7.8 fusion.13
  1208.5 8.7 copy.37
  1217.2 7.2 convolution_bitcast_fusion
  1226.1 6.5 copy.39
  1236.7 4.7 maximum_bitcast_fusion
  1241.4 5.1 gather_fusion.1
  1246.5 10.0 fusion.44
  1257.8 8.3 fusion.67
  1266.1 6.2 fusion.28
  1272.2 26.4 %reduce-scatter.14.cloned.1.call-done = f32[1,8,128,128]{3,2,1,0:T(8,128)} async-done(((f32[1,64,128,128]{3,2,1,0:T(8,128)}), f32[1,8,128,128]{3,2,1,0:T(8,128)}) %reduce-scatter.14.cloned.1.call-update) | async-done | bytes 524304 | tf_op jit(solution)/shard_map/reduce_scatter | solution.py:225
  1306.0 139.6 %reduce-scatter.12.cloned.1.call-done = f32[1024,512]{1,0:T(8,128)} async-done(((f32[4096,512]{1,0:T(8,128)}), f32[1024,512]{1,0:T(8,128)}) %reduce-scatter.12.cloned.1.call-update) | async-done | bytes 2097168 | tf_op jit(solution)/shard_map/reduce_scatter | solution.py:128
  1448.4 46.0 %all-reduce.45 = (f32[2,512]{1,0:T(2,128)S(1)}, f32[]{:T(128)}) all-reduce(f32[2,512]{1,0:T(2,128)S(1)} %pad_maximum_fusion.20, f32[]{:T(128)} %fusion.28), channel_id=1, replica_groups=mesh['dp'=8,'mp'=4] {'dp','mp'}, use_global_device_ids=true, to_apply=%region_13.14 | all-reduce | flops 1025 | bytes 8200 | tf_op jit(solution)/shard_map/psum | solution.py:221
  1495.7 98.4 %reduce-scatter.8.cloned.1.call-done = f32[1024,512]{1,0:T(8,128)} async-done(((f32[4096,512]{1,0:T(8,128)}), f32[1024,512]{1,0:T(8,128)}) %reduce-scatter.8.cloned.1.call-update) | async-done | bytes 2097168 | tf_op jit(solution)/shard_map/reduce_scatter | solution.py:108
  1594.1 5.2 fusion.34
  (364 shorter events, 228.2 us)
Async XLA Ops:
  7.2 1293.8 %copy-start = (f32[1,8,128,128]{3,2,1,0:T(8,128)S(1)}, f32[1,8,128,128]{3,2,1,0:T(8,128)}, u32[]{:S(2)}) copy-start(f32[1,8,128,128]{3,2,1,0:T(8,128)} %param.17) | copy-start | bytes 1572868
  7.2 6.9 copy-start.42
  7.2 34.0 %all-gather.8.cloned.1.call-start = ((), (), s32[]{:S(2)}) async-start(), calls=%async_computation.6 | async-start | bytes 2359296 | tf_op jit(solution)/shard_map/all_gather | solution.py:168
  9.1 115.0 %all-gather.6.cloned.1.call-start = ((), (), s32[]{:S(2)}) async-start(), calls=%async_computation.5 | async-start | bytes 5242880 | tf_op jit(solution)/shard_map/all_gather | solution.py:103
  10.7 30.5 %copy-start.32 = (f32[1024]{0:T(1024)}, f32[1024]{0:T(1024)S(1)}, u32[]{:S(2)}) copy-start(f32[1024]{0:T(1024)S(1)} %fusion.35) | copy-start | bytes 12292
  10.7 30.5 %copy-start.30 = (f32[1024]{0:T(1024)}, f32[1024]{0:T(1024)S(1)}, u32[]{:S(2)}) copy-start(f32[1024]{0:T(1024)S(1)} %fusion.93) | copy-start | bytes 12292
  11.5 29.7 %copy-start.34 = (f32[1,512]{1,0:T(1,128)}, f32[1,512]{1,0:T(1,128)S(1)}, u32[]{:S(2)}) copy-start(f32[1,512]{1,0:T(1,128)S(1)} %get-tuple-element.80) | copy-start | bytes 6148
  14.0 439.9 %reduce-scatter.6.cloned.1.call-start = ((), (), s32[]{:S(2)}) async-start(), calls=%async_computation.7 | async-start | bytes 10485760 | tf_op jit(solution)/shard_map/reduce_scatter | solution.py:108
  16.1 2.0 copy-start.43
  45.9 4.4 copy-start.24
  50.3 73.8 %slice-start = ((bf16[1,512,1280]{1,2,0:T(8,128)(2,1)}), bf16[1,512,768]{1,2,0:T(8,128)(2,1)S(1)}, s32[]{:S(2)}) async-start(bf16[1,512,1280]{1,2,0:T(8,128)(2,1)} %reshape.175), calls=%async_computation.15 | async-start | bytes 1572864 | tf_op jit(solution)/shard_map/slice | solution.py:53
  129.4 4.6 copy-start.1
  280.4 3.4 copy-start.9
  280.4 3.4 copy-start.17
  280.4 4.2 copy-start.18
  286.7 9.4 copy-start.15
  302.3 4.0 copy-start.20
  306.2 4.5 copy-start.13
  310.8 228.3 %all-gather.10.cloned.1.call-start = ((), (), s32[]{:S(2)}) async-start(), calls=%async_computation.8 | async-start | bytes 5242880 | tf_op jit(solution)/shard_map/all_gather | solution.py:103
  457.4 162.4 %all-gather.12.cloned.1.call-start = ((), (), s32[]{:S(2)}) async-start(), calls=%async_computation.10 | async-start | bytes 5242880 | tf_op jit(solution)/shard_map/all_gather | solution.py:117
  458.0 321.8 %reduce-scatter.10.cloned.1.call-start = ((), (), s32[]{:S(2)}) async-start(), calls=%async_computation.11 | async-start | bytes 10485760 | tf_op jit(solution)/shard_map/reduce_scatter | solution.py:128
  619.8 11.2 copy-start.19
  629.0 2.0 copy-start.4
  636.6 253.7 %all-gather.14.cloned.1.call-start = ((), (), s32[]{:S(2)}) async-start(), calls=%async_computation.12 | async-start | bytes 5242880 | tf_op jit(solution)/shard_map/all_gather | solution.py:117
  779.7 2.9 copy-start.7
  779.7 2.9 copy-start.14
  782.7 1.7 copy-start.44
  784.3 514.4 %reduce-scatter.14.cloned.1.call-start = ((), (), s32[]{:S(2)}) async-start(), calls=%async_computation.14 | async-start | bytes 4718592 | tf_op jit(solution)/shard_map/reduce_scatter | solution.py:225
  875.8 6.3 copy-start.5
  875.8 7.4 copy-start.11
  883.3 3.3 copy-start.3
  883.3 3.7 copy-start.12
  893.8 2.0 copy-start.6
  1060.9 4.2 copy-start.23
  1069.2 21.1 %copy-start.29 = (f32[4,15,256]{2,1,0:T(8,128)S(1)}, f32[4,15,256]{2,1,0:T(8,128)}, u32[]{:S(2)}) copy-start(f32[4,15,256]{2,1,0:T(8,128)} %slice.648) | copy-start | bytes 184324
  1094.2 9.8 copy-start.37
  1110.9 5.1 copy-start.36
  1127.3 4.0 copy-start.8
  1127.3 4.0 copy-start.10
  1127.3 4.9 copy-start.16
  1193.0 4.6 copy-start.2
  1217.2 7.2 copy-start.22
  1246.5 199.2 %reduce-scatter.12.cloned.1.call-start = ((), (), s32[]{:S(2)}) async-start(), calls=%async_computation.13 | async-start | bytes 10485760 | tf_op jit(solution)/shard_map/reduce_scatter | solution.py:128
  1256.6 1.2 copy-start.21
  1256.6 337.5 %reduce-scatter.8.cloned.1.call-start = ((), (), s32[]{:S(2)}) async-start(), calls=%async_computation.9 | async-start | bytes 10485760 | tf_op jit(solution)/shard_map/reduce_scatter | solution.py:108
  1272.2 31.7 %copy-start.25 = (f32[1,8,128,128]{3,2,1,0:T(8,128)S(1)}, f32[1,8,128,128]{3,2,1,0:T(8,128)}, u32[]{:S(2)}) copy-start(f32[1,8,128,128]{3,2,1,0:T(8,128)} %param.13) | copy-start | bytes 1572868
  1298.7 4.3 copy-start.26
  1300.9 144.7 %copy-start.31 = (f32[1024]{0:T(1024)S(1)}, f32[1024]{0:T(1024)}, u32[]{:S(2)}) copy-start(f32[1024]{0:T(1024)} %copy-done.30) | copy-start | bytes 12292
  1301.0 144.7 %copy-start.35 = (f32[1,512]{1,0:T(1,128)S(1)}, f32[1,512]{1,0:T(1,128)}, u32[]{:S(2)}) copy-start(f32[1,512]{1,0:T(1,128)} %copy-done.34) | copy-start | bytes 6148
  1302.9 1.0 copy-start.27
  1302.9 1.0 copy-start.28
  1302.9 145.4 %copy-start.39 = (f32[512]{0:T(512)S(1)}, f32[512]{0:T(512)}, u32[]{:S(2)}) copy-start(f32[512]{0:T(512)} %get-tuple-element.14) | copy-start | bytes 6148
  1302.9 192.1 %copy-start.33 = (f32[1024]{0:T(1024)S(1)}, f32[1024]{0:T(1024)}, u32[]{:S(2)}) copy-start(f32[1024]{0:T(1024)} %copy-done.32) | copy-start | bytes 12292
  1303.0 192.1 %copy-start.38 = (f32[2,512]{1,0:T(2,128)S(1)}, f32[2,512]{1,0:T(2,128)}, u32[]{:S(2)}) copy-start(f32[2,512]{1,0:T(2,128)} %param.19) | copy-start | bytes 12292
  1303.0 192.1 %copy-start.40 = (f32[2,512]{1,0:T(2,128)S(1)}, f32[2,512]{1,0:T(2,128)}, u32[]{:S(2)}) copy-start(f32[2,512]{1,0:T(2,128)} %param.21) | copy-start | bytes 12292
  1303.0 192.1 %copy-start.41 = (f32[2,512]{1,0:T(2,128)S(1)}, f32[2,512]{1,0:T(2,128)}, u32[]{:S(2)}) copy-start(f32[2,512]{1,0:T(2,128)} %param.20) | copy-start | bytes 12292
Sparse Core Ops, SparseCore 0:
  10.5 30.6 all-gather.7
  43.3 80.7 all-gather.5
  310.9 142.9 reduce-scatter.5
  457.5 81.4 all-gather.9
  540.4 79.2 all-gather.11
  636.7 142.9 reduce-scatter.9
  784.4 81.4 all-gather.13
  1246.6 52.0 reduce-scatter.13
  1301.1 144.4 reduce-scatter.11
  1448.0 146.1 reduce-scatter.7
where the time goes:
time: 1640 us; the launch traced here: 1610 us
  waiting for transfers between devices  785 us (48%)
  local copies, waits for them, and re-layouts  526 us (32%)
  other arithmetic  137 us (8%)
  matrix products  94.8 us (6%)
  blocking collectives  46 us (3%)
  between operations  17.7 us (1%)
    reduce_scatter x2, waiting for transfers between devices, collect_rows(): lax.psum_scatter(lax.dot_general(grad_low, weight, (((1,), (1,)), ((), ()...  283 us
    slice x66, local copies, waits for them, and re-layouts, on_device(): lax.associative_scan(combine_steps, (keep_next, d_state.reshape(seq_count...  253 us
    reduce_scatter x2, waiting for transfers between devices, reduce_rows(): lax.psum_scatter(jnp.dot(activation, weight, preferred_element_type=jnp.f...  241 us
    all_gather x2, waiting for transfers between devices, project_rows(): lax.all_gather(normed, 'mp', axis=0, tiled=True)  153 us
    slice x60, local copies, waits for them, and re-layouts, on_device(): lax.associative_scan(combine_steps, (keep_seq, write_term.reshape(seq_cou...  115 us
    all_gather x2, waiting for transfers between devices, spread_grads(): shard_rows = lax.all_gather(grad_low, 'mp', axis=0, tiled=True)  57.5 us
    psum x1, blocking collectives, on_device(): gain_grad = lax.psum(gain_local, ('dp', 'mp'))  46 us
    pad x18, local copies, waits for them, and re-layouts, on_device(): lax.associative_scan(combine_steps, (keep_next, d_state.reshape(seq_count...  41.5 us
  transfers between devices with their start and end apart: 10, of which 9 were waited for; matrix products, arithmetic and copies ran while one was open for 11% of the time, Pallas kernels for 0%

commit v1 on v0

v1 whole, which is shorter than its diff:
```python
import functools

import jax
import jax.numpy as jnp
from jax import lax
from jax.experimental import pallas as pl
from jax.experimental.pallas import tpu as pltpu
from jax.sharding import PartitionSpec as P

D = 512
H = 1024
FF = 2048
BLK = 128
STEP = 10
L = 1024

norm_eps = 1e-05
beta_one = 0.5
beta_two = 0.5
adam_eps = 1e-08
learn_rate = 0.02
gain_rate = 0.1
weight_decay = 0.1
highest = lax.Precision.HIGHEST

f32 = jnp.float32
bf16 = jnp.bfloat16
SUB = 8
J = L // SUB
R = 256


def dot(a, b, trans_b=False):
    dims = (((1,), (1,)), ((), ())) if trans_b else (((1,), (0,)), ((), ()))
    return lax.dot_general(a, b, dims, preferred_element_type=f32)


def recip(v):
    return pltpu.reciprocal(v, approx=True)


def sigmoid(v):
    return recip(1.0 + jnp.exp(-v))


def shift_down(v):
    rolled = pltpu.roll(v, 1, 0)
    row = lax.broadcasted_iota(jnp.int32, v.shape, 0)
    return jnp.where(row == 0, 0.0, rolled)


def shift_up(v):
    rolled = pltpu.roll(v, SUB - 1, 0)
    row = lax.broadcasted_iota(jnp.int32, v.shape, 0)
    return jnp.where(row == SUB - 1, 0.0, rolled)


def gelu_terms(x):
    a = jnp.abs(x)
    t = recip(1.0 + a * (0.3275911 * 0.7071067811865476))
    poly = t * (
        0.5 * 0.254829592
        + t
        * (
            0.5 * -0.284496736
            + t * (0.5 * 1.421413741 + t * (0.5 * -1.453152027 + t * (0.5 * 1.061405429)))
        )
    )
    e = jnp.exp(x * x * -0.5)
    tail = poly * e
    cdf = jnp.where(x < 0.0, tail, 1.0 - tail)
    return cdf, x * e * 0.3989422804014327


def compute_kernel(
    tokens,
    cotangent,
    wg,
    wu,
    wo,
    wd,
    gains,
    block_out,
    input_grad,
    gg,
    gu,
    go,
    gd,
    small,
    n1,
    n1t,
    cot,
    cott,
    n2,
    n2t,
    dml,
    dmlt,
    forget,
    admit,
    cand,
    state,
    scan,
    acc_a,
    acc_b,
    mixed,
    act,
    dup,
    dpre,
    fills,
):
    parts, _, hm3 = wg.shape
    hm = hm3 // 3
    fm = wu.shape[2]
    gain_one = gains[0:1, :]
    gain_two = gains[1:2, :]

    def permute_in(src, dst):
        for k in range(D // BLK):
            scan[k] = src[:, k * BLK : (k + 1) * BLK].astype(f32)

        @pl.loop(0, J // 2, unroll=4)
        def _(j):
            for k in range(D // BLK):
                lo = scan[k, pl.ds(2 * j, SUB, stride=J), :]
                hi = scan[k, pl.ds(2 * j + 1, SUB, stride=J), :]
                dst[pl.ds(pl.multiple_of(16 * j, 16), 16), k * BLK : (k + 1) * BLK] = jnp.concatenate([lo, hi], 0).astype(bf16)

    def permute_out(src, dst):
        @pl.loop(0, J, unroll=4)
        def _(j):
            rows = pl.ds(pl.multiple_of(j * SUB, SUB), SUB)
            for k in range(D // BLK):
                scan[k, pl.ds(j, SUB, stride=J), :] = src[rows, k * BLK : (k + 1) * BLK]

        for k in range(D // BLK):
            dst[:, k * BLK : (k + 1) * BLK] = scan[k].astype(dst.dtype)

    def put(first, rows, value):
        for k in range(hm // BLK):
            scan[first + k, rows, :] = value[:, k * BLK : (k + 1) * BLK]

    def take(first, rows):
        return jnp.concatenate([scan[first + k, rows, :] for k in range(hm // BLK)], 1)

    half = hm // BLK

    permute_in(cotangent, cot)
    cott[...] = cot[...].T
    permute_in(tokens, n1)
    mixed[...] = n1[...].astype(f32)

    @pl.loop(0, L // R)
    def _(i):
        rows = pl.ds(pl.multiple_of(i * R, R), R)
        x = mixed[rows, :]
        r = lax.rsqrt(jnp.mean(x * x, axis=-1, keepdims=True) + norm_eps)
        n1[rows, :] = (x * r * gain_one).astype(bf16)

    n1t[...] = n1[...].T

    fills[0] = jnp.zeros((SUB, hm), f32)
    fills[1] = jnp.ones((SUB, hm), f32)
    weigh = fills[0]
    weigh_j = fills[0]
    for m in range(parts):

        @pl.loop(0, L // R)
        def _(i):
            rows = pl.ds(pl.multiple_of(i * R, R), R)
            x = n1[rows, :]
            forget[m, rows, :] = dot(x, wg[m, :, :hm])
            admit[m, rows, :] = dot(x, wg[m, :, hm : 2 * hm])
            cand[m, rows, :] = dot(x, wg[m, :, 2 * hm :])

        def step(j, carry):
            s, p, k_sum, kj_sum = carry
            rows = pl.ds(pl.multiple_of(j * SUB, SUB), SUB)
            f = sigmoid(forget[m, rows, :])
            a = sigmoid(admit[m, rows, :])
            inv = recip(f + a)
            keep = f * inv
            s = keep * s + a * inv * cand[m, rows, :]
            p = keep * p
            forget[m, rows, :] = f
            admit[m, rows, :] = a
            put(0, rows, s)
            put(half, rows, p)
            return s, p, k_sum + keep, kj_sum + keep * j.astype(f32)

        s, p, weigh, weigh_j = lax.fori_loop(
            0,
            J,
            step,
            (fills[0], fills[1], weigh, weigh_j),
            unroll=4,
        )
        enter = fills[0]
        for _ in range(SUB - 1):
            enter = shift_down(s + p * enter)

        @pl.loop(0, J, unroll=4)
        def _(j):
            rows = pl.ds(pl.multiple_of(j * SUB, SUB), SUB)
            state[m, rows, :] = take(0, rows) + take(half, rows) * enter

        @pl.loop(0, L // R)
        def _(i):
            rows = pl.ds(pl.multiple_of(i * R, R), R)
            mixed[rows, :] += dot(state[m, rows, :].astype(bf16), wo[m])

    @pl.loop(0, L // R)
    def _(i):
        rows = pl.ds(pl.multiple_of(i * R, R), R)
        x = mixed[rows, :]
        r = lax.rsqrt(jnp.mean(x * x, axis=-1, keepdims=True) + norm_eps)
        n2[rows, :] = (x * r * gain_two).astype(bf16)
        acc_a[rows, :] = x
        acc_b[rows, :] = jnp.zeros_like(x)

    n2t[...] = n2[...].T

    for m in range(parts):

        @pl.loop(0, L // R)
        def _(i):
            rows = pl.ds(pl.multiple_of(i * R, R), R)
            up = dot(n2[rows, :], wu[m])
            da = dot(cot[rows, :], wd[m], True)
            cdf, xpdf = gelu_terms(up)
            ac = (up * cdf).astype(bf16)
            du = (da * (cdf + xpdf)).astype(bf16)
            act[rows, :] = ac
            dup[rows, :] = du
            acc_a[rows, :] += dot(ac, wd[m])
            acc_b[rows, :] += dot(du, wu[m], True)

        gd[m] = dot(cott[...], act[...]).astype(gd.dtype)
        gu[m] = dot(n2t[...], dup[...]).astype(gu.dtype)

    permute_out(acc_a, block_out)

    gain_sum_two = jnp.zeros((1, D), f32)

    def back_two(i, total):
        rows = pl.ds(pl.multiple_of(i * R, R), R)
        x = mixed[rows, :]
        r = lax.rsqrt(jnp.mean(x * x, axis=-1, keepdims=True) + norm_eps)
        dn = acc_b[rows, :]
        q = dn * gain_two
        d = cot[rows, :].astype(f32) + r * q - r * r * r * x * jnp.mean(q * x, axis=-1, keepdims=True)
        mixed[rows, :] = d
        dml[rows, :] = d.astype(bf16)
        acc_b[rows, :] = jnp.zeros_like(d)
        return total + jnp.sum(dn * x * r, axis=0, keepdims=True)

    gain_sum_two = lax.fori_loop(0, L // R, back_two, gain_sum_two)
    dmlt[...] = dml[...].T

    for m in range(parts):

        @pl.loop(0, L // R)
        def _(i):
            rows = pl.ds(pl.multiple_of(i * R, R), R)
            put(0, rows, dot(dml[rows, :], wo[m], True))

        def step(k, carry):
            u, p, keep_next = carry
            j = J - 1 - k
            rows = pl.ds(pl.multiple_of(j * SUB, SUB), SUB)
            u = take(0, rows) + keep_next * u
            p = keep_next * p
            put(0, rows, u)
            put(half, rows, p)
            f = forget[m, rows, :]
            return u, p, f * recip(f + admit[m, rows, :])

        u, p, keep_first = lax.fori_loop(
            0,
            J,
            step,
            (fills[0], fills[1], fills[1]),
            unroll=4,
        )
        enter = fills[0]
        for _ in range(SUB - 1):
            enter = shift_up(keep_first * (u + p * enter))

        def back(i, before):
            parts_out = []
            for h in range(2):
                rows = pl.ds(pl.multiple_of(i * 2 * SUB + h * SUB, SUB), SUB)
                carried = take(0, rows) + take(half, rows) * enter
                f = forget[m, rows, :]
                a = admit[m, rows, :]
                inv = recip(f + a)
                adm = a * inv
                g = carried * (before - cand[m, rows, :]) * (f * inv * adm)
                parts_out.append((g * (1.0 - f), g * (a - 1.0), carried * adm))
                before = state[m, rows, :]
            both = pl.ds(pl.multiple_of(i * 2 * SUB, 2 * SUB), 2 * SUB)
            for k in range(3):
                dpre[both, k * hm : (k + 1) * hm] = jnp.concatenate(
                    [parts_out[0][k], parts_out[1][k]], 0
                ).astype(bf16)
            return before

        last = state[m, pl.ds(L - SUB, SUB), :]
        lax.fori_loop(0, J // 2, back, shift_down(last), unroll=2)

        gg[m] = dot(n1t[...], dpre[...]).astype(gg.dtype)
        go[m] = dot(dmlt[...], state[m].astype(bf16)).astype(go.dtype)

        @pl.loop(0, L // R)
        def _(i):
            rows = pl.ds(pl.multiple_of(i * R, R), R)
            acc_b[rows, :] += dot(dpre[rows, :], wg[m], True)

    permute_in(tokens, n1)

    def back_one(i, total):
        rows = pl.ds(pl.multiple_of(i * R, R), R)
        x = n1[rows, :].astype(f32)
        r = lax.rsqrt(jnp.mean(x * x, axis=-1, keepdims=True) + norm_eps)
        dn = acc_b[rows, :]
        q = dn * gain_one
        mixed[rows, :] += r * q - r * r * r * x * jnp.mean(q * x, axis=-1, keepdims=True)
        return total + jnp.sum(dn * x * r, axis=0, keepdims=True)

    gain_sum_one = lax.fori_loop(0, L // R, back_one, jnp.zeros((1, D), f32))

    permute_out(mixed, input_grad)

    place = lax.broadcasted_iota(jnp.int32, (SUB, hm), 0).astype(f32) * float(J)
    small[...] = jnp.zeros_like(small)
    small[0:1, :] = gain_sum_one
    small[1:2, :] = gain_sum_two
    small[2:3, :hm] = jnp.sum(weigh, axis=0, keepdims=True)
    small[3:4, :hm] = jnp.sum(weigh_j + weigh * place, axis=0, keepdims=True)


def compute(tokens, cotangent, wg, wu, wo, wd, gains, grad_type):
    parts, _, hm3 = wg.shape
    hm, fm = hm3 // 3, wu.shape[2]
    sds = jax.ShapeDtypeStruct
    vm = pl.BlockSpec(memory_space=pltpu.VMEM)
    return pl.pallas_call(
        compute_kernel,
        out_shape=(
            sds((L, D), bf16),
            sds((L, D), f32),
            sds((parts, D, 3 * hm), grad_type),
            sds((parts, D, fm), grad_type),
            sds((parts, D, hm), grad_type),
            sds((parts, D, fm), grad_type),
            sds((8, D), f32),
        ),
        in_specs=[vm] * 7,
        out_specs=[vm] * 7,
        scratch_shapes=[
            pltpu.VMEM((L, D), bf16),
            pltpu.VMEM((D, L), bf16),
            pltpu.VMEM((L, D), bf16),
            pltpu.VMEM((D, L), bf16),
            pltpu.VMEM((L, D), bf16),
            pltpu.VMEM((D, L), bf16),
            pltpu.VMEM((L, D), bf16),
            pltpu.VMEM((D, L), bf16),
            pltpu.VMEM((parts, L, hm), f32),
            pltpu.VMEM((parts, L, hm), f32),
            pltpu.VMEM((parts, L, hm), f32),
            pltpu.VMEM((parts, L, hm), f32),
            pltpu.VMEM((2 * hm // BLK, L, BLK), f32),
            pltpu.VMEM((L, D), f32),
            pltpu.VMEM((L, D), f32),
            pltpu.VMEM((L, D), f32),
            pltpu.VMEM((L, fm), bf16),
            pltpu.VMEM((L, fm), bf16),
            pltpu.VMEM((L, 3 * hm), bf16),
            pltpu.VMEM((2, SUB, hm), f32),
        ],
        compiler_params=pltpu.CompilerParams(vmem_limit_bytes=63 * 2**20),
        name="block",
    )(tokens, cotangent, wg, wu, wo, wd, gains)


def adam_update(first_old, second_old, gradient):
    first_new = beta_one * first_old + (1.0 - beta_one) * gradient
    second_new = beta_two * second_old + (1.0 - beta_two) * gradient * gradient
    first_hat = first_new / (1.0 - beta_one**STEP)
    second_hat = second_new / (1.0 - beta_two**STEP)
    return (first_new, second_new, first_hat / (jnp.sqrt(second_hat) + adam_eps))


def soap_update(master, moment_one, moment_two, basis_left, basis_right, grads):
    left_side = jnp.einsum("pkab,pkac->pkbc", basis_left, grads, precision=highest)
    rotated = jnp.einsum("pkbc,pkcd->pkbd", left_side, basis_right, precision=highest)
    first_new, second_new, direction = adam_update(moment_one, moment_two, rotated)
    turned = jnp.einsum("pkab,pkbc->pkac", basis_left, direction, precision=highest)
    turned = jnp.einsum("pkac,pkdc->pkad", turned, basis_right, precision=highest)
    master_new = master - learn_rate * (turned + weight_decay * master)
    return (first_new, second_new, master_new)


def on_device(
    tokens,
    cotangent,
    master,
    moment_one,
    moment_two,
    basis_left,
    basis_right,
    owner,
    gains,
    gain_moment_one,
    gain_moment_two,
):
    parts = lax.axis_size("mp")
    data_parts = lax.axis_size("dp")
    hm, fm = H // parts, FF // parts
    token_total = L * data_parts * parts
    row_tiles, cols, lows = D // BLK, (3 * hm + fm) // BLK, (hm + fm) // BLK
    slot_order = jnp.argsort(owner, stable=True)
    block_rank = jnp.argsort(slot_order, stable=True)
    stored = lax.all_gather(master.astype(bf16), "dp", axis=1, tiled=True)
    stored = lax.all_gather(stored, "mp", axis=0, tiled=True)
    stack = stored[:, block_rank]
    upper = stack[:, : row_tiles * cols].reshape(parts, row_tiles, cols, BLK, BLK)
    upper = upper.transpose(0, 1, 3, 2, 4).reshape(parts, D, cols * BLK)
    lower = stack[:, row_tiles * cols :].reshape(parts, lows, row_tiles, BLK, BLK)
    lower = lower.transpose(0, 1, 3, 2, 4).reshape(parts, lows * BLK, D)
    block_out, input_grad, gg, gu, go, gd, small = compute(
        tokens, cotangent, upper[:, :, : 3 * hm], upper[:, :, 3 * hm :], lower[:, :hm], lower[:, hm:], gains, bf16
    )
    upper = jnp.concatenate([gg, gu], axis=2).reshape(parts, row_tiles, BLK, cols, BLK).transpose(0, 1, 3, 2, 4)
    upper = upper.reshape(parts, row_tiles * cols, BLK, BLK)
    lower = jnp.concatenate([go, gd], axis=2).reshape(parts, row_tiles, BLK, lows, BLK).transpose(0, 3, 1, 4, 2)
    lower = lower.reshape(parts, row_tiles * lows, BLK, BLK)
    natural = jnp.concatenate([upper, lower], axis=1).astype(f32)
    owned = lax.psum_scatter(natural[:, slot_order], "dp", scatter_dimension=1, tiled=True)
    owned = lax.psum_scatter(owned, "mp", scatter_dimension=0, tiled=True)
    first_new, second_new, master_new = soap_update(master, moment_one, moment_two, basis_left, basis_right, owned)
    first_row = (lax.axis_index("dp") * parts + lax.axis_index("mp")) * L
    forget_part = (jnp.sum(small[3, :hm]) + (first_row + 1).astype(f32) * jnp.sum(small[2, :hm])) / float(token_total)
    gain_grad, forget_total = lax.psum((small[:2], forget_part), ("dp", "mp"))
    gain_first, gain_second, gain_direction = adam_update(gain_moment_one, gain_moment_two, gain_grad)
    gains_new = gains - gain_rate * gain_direction
    forget_mean = forget_total / (H * (token_total + 1) / 2.0)
    return (
        block_out,
        input_grad,
        first_new,
        second_new,
        master_new,
        master_new.astype(bf16),
        gain_first,
        gain_second,
        gains_new,
        forget_mean,
    )


def solution(mesh):
    rows, blocks = P(("dp", "mp"), None), P("mp", "dp", None, None)
    return jax.shard_map(
        on_device,
        mesh=mesh,
        in_specs=(rows, rows, blocks, blocks, blocks, blocks, blocks, P(), P(), P(), P()),
        out_specs=(rows, rows, blocks, blocks, blocks, blocks, P(), P(), P(), P()),
        check_vma=False,
    )
```

time: 1640 us -> 635 us (0.39); the launches traced: 1610 us -> 633 us
  waiting for transfers between devices: 785 us -> 334 us
  local copies, waits for them, and re-layouts: 526 us -> 118 us
  other arithmetic: 137 us -> 25.2 us
  Pallas kernels: 0 us -> 88.5 us
  matrix products: 94.8 us -> 6.43 us
    reduce_scatter x4 -> x0, waiting for transfers between devices: 524 us -> none  [the longest x2 283 us: collect_rows(): lax.psum_scatter(lax.dot_general(grad_low, weight, (((1,), (1,)), ((), ()...]
    slice x132 -> x8, local copies, waits for them, and re-layouts: 373 us -> 19.2 us  [the longest x1 6.9 us: on_device(): stack[:, :row_tiles * cols].reshape(parts, row_tiles, cols, BLK, BLK)]
    pallas_call x0 -> x1, Pallas kernels: none -> 88.5 us  [compute(): pl.pallas_call(compute_kernel, out_shape=(sds((L, D), bf16), sds((L, D),...]
    reduce_scatter x1, waiting for transfers between devices: 26.4 us -> 114 us  [on_device(): lax.psum_scatter(natural[:, slot_order], 'dp', scatter_dimension=1, tiled...]
    dot_general x12 -> x0, matrix products: 87.6 us -> none  [the longest x2 28.6 us: project_rows(): jnp.dot(lax.all_gather(normed, 'mp', axis=0, tiled=True), weight, preferr...]
    pad x36 -> x0, local copies, waits for them, and re-layouts: 67.4 us -> none  [the longest x18 41.5 us: on_device(): lax.associative_scan(combine_steps, (keep_next, d_state.reshape(seq_count...]
    all_gather x5 -> x2, waiting for transfers between devices: 234 us -> 178 us  [the longest x1 146 us: on_device(): stored = lax.all_gather(stored, 'mp', axis=0, tiled=True)]
    add x40 -> x0, other arithmetic: 44 us -> none  [the longest x10 16.1 us: on_device(): lax.associative_scan(combine_steps, (keep_next, d_state.reshape(seq_count...]
  transfers between devices with their start and end apart: 10 -> 4, of which waited for: 9 -> 4; matrix products, arithmetic and copies ran while one was open for 11% -> 1% of each run, Pallas kernels for 0% -> 0%
where the time goes in v1:
time: 635 us; the launch traced here: 633 us
  waiting for transfers between devices  334 us (53%)
  local copies, waits for them, and re-layouts  118 us (19%)
  Pallas kernels  88.5 us (14%)
  blocking collectives  43.2 us (7%)
  other arithmetic  25.2 us (4%)
  between operations  17.1 us (3%)
  matrix products  6.43 us (1%)
    all_gather x1, waiting for transfers between devices, on_device(): stored = lax.all_gather(stored, 'mp', axis=0, tiled=True)  146 us
    reduce_scatter x1, waiting for transfers between devices, on_device(): lax.psum_scatter(natural[:, slot_order], 'dp', scatter_dimension=1, tiled...  114 us
    pallas_call x1, Pallas kernels, compute(): pl.pallas_call(compute_kernel, out_shape=(sds((L, D), bf16), sds((L, D),...  88.5 us
    psum x1, blocking collectives, on_device(): gain_grad, forget_total = lax.psum((small[:2], forget_part), ('dp', 'mp'))  43.2 us
    unnamed x5, waiting for transfers between devices  41.3 us
    all_gather x1, waiting for transfers between devices, on_device(): stored = lax.all_gather(master.astype(bf16), 'dp', axis=1, tiled=True)  32 us
    gather x1, local copies, waits for them, and re-layouts, on_device(): natural[:, slot_order]  14.6 us
  transfers between devices with their start and end apart: 4, of which 4 were waited for; matrix products, arithmetic and copies ran while one was open for 1% of the time, Pallas kernels for 0%

profile of v1, /device:TPU:0, one launch (start us, length us, event | category | flops | bytes accessed | tf_op | source)
XLA Modules:
  0.0 633.1 jit_solution(8917416032264909826)
XLA Ops:
  7.2 0.0 copy-start
  7.2 0.0 all-gather.3.cloned.1.call-start
  7.2 1.8 bitcast_convert_fusion
  9.1 0.0 all-gather.3.cloned.1.call-update
  9.1 0.0 all-gather.5.cloned.1.call-start
  9.1 32.0 %all-gather.3.cloned.1.call-done = bf16[1,64,128,128]{3,2,0,1:T(8,128)(2,1)} async-done(((bf16[1,8,128,128]{3,2,0,1:T(8,128)(2,1)}), bf16[1,64,128,128]{3,2,0,1:T(8,128)(2,1)}) %all-gather.3.cloned.1.call-update) | async-done | bytes 2097168 | tf_op jit(solution)/shard_map/all_gather | solution.py:424
  41.1 0.0 all-gather.5.cloned.1.call-update
  41.1 0.0 reduce-scatter.5.cloned.1.call-start
  41.2 2.7 sort.31
  43.9 2.0 sort.32
  46.0 146.4 %all-gather.5.cloned.1.call-done = bf16[4,64,128,128]{3,2,1,0:T(8,128)(2,1)} async-done(((bf16[1,64,128,128]{3,2,1,0:T(8,128)(2,1)}), bf16[4,64,128,128]{3,2,1,0:T(8,128)(2,1)}) %all-gather.5.cloned.1.call-update) | async-done | bytes 8388624 | tf_op jit(solution)/shard_map/all_gather | solution.py:425
  192.3 8.9 %gather_fusion = bf16[64,4,128,128]{3,2,1,0:T(8,128)(2,1)} fusion(bf16[4,64,128,128]{3,2,1,0:T(8,128)(2,1)} %all-gather.5.cloned.1.call-done, s32[1024]{0:T(1024)S(1)} %pad_clamp_fusion.1), kind=kCustom, calls=%fused_computation | custom fusion | bytes 16777472 | tf_op jit(solution)/shard_map/gather | solution.py:426
  201.3 2.1 slice.43
  203.4 6.9 %slice.40 = bf16[4,40,128,128]{3,2,0,1:T(8,128)(2,1)} slice(bf16[4,64,128,128]{3,2,0,1:T(8,128)(2,1)} %bitcast.68), slice={[0:4], [0:40], [0:128], [0:128]} | slice | bytes 10485760 | tf_op jit(solution)/shard_map/slice | solution.py:427
  210.3 4.6 copy.54
  214.9 5.7 reshape.71
  220.6 2.3 slice.44.wo
  222.9 3.1 slice.45.wd
  226.0 9.0 %copy.33 = bf16[4,4,10,128,128]{3,1,4,2,0:T(4,128)(2,1)} copy(bf16[4,4,10,128,128]{4,3,0,2,1:T(8,128)(2,1)} %bitcast.69) | data formatting | bytes 10485760 | tf_op jit(solution)/shard_map/reshape | solution.py:427
  235.0 8.7 %reshape.69 = bf16[4,512,1280]{1,2,0:T(8,128)(2,1)} reshape(bf16[4,4,128,10,128]{2,1,4,3,0:T(4,128)(2,1)} %bitcast.70) | data formatting | bytes 10485760 | tf_op jit(solution)/shard_map/reshape | solution.py:428
  243.7 4.0 slice.41
  247.7 4.7 copy.51.wg
  252.4 0.0 slice-done
  252.4 2.4 copy.52.wu
  254.8 88.5 %block.1 = (bf16[1024,512]{1,0:T(8,128)(2,1)}, f32[1024,512]{1,0:T(8,128)}, bf16[4,512,768]{2,1,0:T(8,128)(2,1)}, bf16[4,512,512]{2,1,0:T(8,128)(2,1)}, bf16[4,5...) custom-call(bf16[1024,512]{1,0:T(8,128)(2,1)} %tokens.1, bf16[1024,512]{1,0:T(8,128)(2,1)} %cotangent.1, ...), custom_call_target="tpu_custom_call" | custom-call | tf_op jit(solution)/shard_map/block/pallas_call | solution.py:346
  343.3 3.7 pad_maximum_fusion.1
  347.0 4.7 copy.39
  351.8 5.6 reshape.74
  357.4 4.6 copy.40
  362.0 0.0 copy-done.2
  362.0 0.0 copy-done.1
  362.0 2.7 pad_maximum_fusion
  364.7 7.9 %copy.37 = bf16[4,512,1280]{1,2,0:T(8,128)(2,1)} copy(bf16[4,512,1280]{2,1,0:T(8,128)(2,1)} %pad_maximum_fusion) | data formatting | bytes 10485760 | tf_op jit(solution)/shard_map/concatenate | solution.py:434
  372.6 8.3 %reshape.72 = bf16[4,4,128,10,128]{2,1,4,3,0:T(4,128)(2,1)} reshape(bf16[4,512,1280]{1,2,0:T(8,128)(2,1)} %copy.37) | data formatting | bytes 10485760 | tf_op jit(solution)/shard_map/reshape | solution.py:434
  380.9 8.9 %copy.38 = bf16[4,4,10,128,128]{4,3,2,1,0:T(8,128)(2,1)} copy(bf16[4,4,10,128,128]{3,1,4,2,0:T(4,128)(2,1)} %bitcast.71) | data formatting | bytes 10485760 | tf_op jit(solution)/shard_map/transpose | solution.py:434
  389.8 10.3 %maximum_convert_fusion = f32[4,64,128,128]{3,2,1,0:T(8,128)} fusion(bf16[4,24,128,128]{3,2,1,0:T(8,128)(2,1)} %bitcast.73, bf16[4,40,128,128]{3,2,1,0:T(8,128)(2,1)} %bitcast.72), kind=kLoop, calls=%fused_computation.2 | loop fusion | flops 8388608 | bytes 25165824 | tf_op jit(solution)/shard_map/convert_element_type | solution.py:438
  400.0 14.6 %gather_fusion.1 = f32[64,4,128,128]{3,2,1,0:T(8,128)} fusion(f32[4,64,128,128]{3,2,1,0:T(8,128)} %maximum_convert_fusion, s32[1024]{0:T(1024)S(1)} %pad_clamp_fusion), kind=kCustom, calls=%fused_computation.1 | custom fusion | bytes 33554688 | tf_op jit(solution)/shard_map/gather | solution.py:439
  414.6 0.0 copy-start.4
  414.7 0.0 copy-start.5
  414.7 0.0 copy-start.6
  414.7 0.0 reduce-scatter.5.cloned.1.call-update
  414.7 0.0 copy-start.3
  414.7 0.0 all-reduce.4.cloned.1.call-start
  414.8 114.3 %reduce-scatter.5.cloned.1.call-done = f32[4,8,128,128]{3,2,0,1:T(8,128)} async-done(((f32[4,64,128,128]{3,2,0,1:T(8,128)}), f32[4,8,128,128]{3,2,0,1:T(8,128)}) %reduce-scatter.5.cloned.1.call-update) | async-done | bytes 2097168 | tf_op jit(solution)/shard_map/reduce_scatter | solution.py:439
  529.1 0.0 all-reduce.4.cloned.1.call-update
  529.1 0.0 copy-done.12
  529.1 0.6 dynamic-slice
  529.7 0.7 slice.33
  530.4 1.4 slice_reduce_fusion
  533.1 43.2 %all-reduce.1 = (f32[2,512]{1,0:T(2,128)S(1)}, f32[]{:T(128)}) all-reduce(f32[2,512]{1,0:T(2,128)S(1)} %slice.33, f32[]{:T(128)S(6)} %div.30), channel_id=1, replica_groups=mesh['dp'=8,'mp'=4] {'dp','mp'}, use_global_device_ids=true, to_apply=%region_4.5 | all-reduce | flops 1025 | bytes 8200 | tf_op jit(solution)/shard_map/psum | solution.py:444
  577.0 0.0 copy-done.9
  577.0 0.0 copy-done.10
  577.0 0.6 multiply_subtract_fusion
  577.6 41.2 %all-reduce.4.cloned.1.call-done = f32[4,8,128,128]{3,2,0,1:T(8,128)} async-done(((f32[4,8,128,128]{3,2,0,1:T(8,128)}), f32[4,8,128,128]{3,2,0,1:T(8,128)}) %all-reduce.4.cloned.1.call-update) | async-done | bytes 2097168
  618.9 0.0 copy-done.4
  618.9 2.7 fusion.6
  621.6 0.0 copy-done
  621.6 0.0 copy-done.5
  621.6 0.0 copy-done.6
  621.6 0.7 fusion.5
  622.4 0.0 copy-start.7
  622.4 0.0 copy-start.8
  622.4 0.9 fusion.7
  623.3 2.1 fusion.26
  (17 shorter events, 0.0 us)
Async XLA Ops:
  7.2 614.4 %copy-start = (f32[1,8,128,128]{3,2,1,0:T(8,128)S(1)}, f32[1,8,128,128]{3,2,1,0:T(8,128)}, u32[]{:S(2)}) copy-start(f32[1,8,128,128]{3,2,1,0:T(8,128)} %param.17) | copy-start | bytes 1572868
  7.2 33.9 %all-gather.3.cloned.1.call-start = ((), (), s32[]{:S(2)}) async-start(), calls=%async_computation.1 | async-start | bytes 2359296 | tf_op jit(solution)/shard_map/all_gather | solution.py:424
  9.1 183.2 %all-gather.5.cloned.1.call-start = ((), (), s32[]{:S(2)}) async-start(), calls=%async_computation.2 | async-start | bytes 10485760 | tf_op jit(solution)/shard_map/all_gather | solution.py:425
  41.1 487.9 %reduce-scatter.5.cloned.1.call-start = ((), (), s32[]{:S(2)}) async-start(), calls=%async_computation.3 | async-start | bytes 18874368 | tf_op jit(solution)/shard_map/reduce_scatter | solution.py:439
  243.7 8.7 %slice-start = ((bf16[4,512,1280]{1,2,0:T(8,128)(2,1)}), bf16[4,512,512]{1,2,0:T(8,128)(2,1)S(1)}, s32[]{:S(2)}) async-start(bf16[4,512,1280]{1,2,0:T(8,128)(2,1)} %reshape.69), calls=%async_computation.5 | async-start | bytes 4194304 | tf_op jit(solution)/shard_map/slice | solution.py:432
  351.8 10.2 %copy-start.2 = (bf16[4,512,512]{2,1,0:T(8,128)(2,1)S(1)}, bf16[4,512,512]{2,1,0:T(8,128)(2,1)}, u32[]{:S(2)}) copy-start(bf16[4,512,512]{2,1,0:T(8,128)(2,1)} %get-tuple-element.24) | copy-start | bytes 6291460
  357.4 4.6 copy-start.1
  414.6 114.5 %copy-start.12 = (u32[32]{0:T(128)S(1)}, u32[32]{0:T(128)}, u32[]{:S(2)}) copy-start(u32[32]{0:T(128)} %constant.52) | copy-start | bytes 388
  414.6 162.4 %copy-start.9 = (f32[2,512]{1,0:T(2,128)S(1)}, f32[2,512]{1,0:T(2,128)}, u32[]{:S(2)}) copy-start(f32[2,512]{1,0:T(2,128)} %gains.1) | copy-start | bytes 12292
  414.6 162.4 %copy-start.10 = (f32[2,512]{1,0:T(2,128)S(1)}, f32[2,512]{1,0:T(2,128)}, u32[]{:S(2)}) copy-start(f32[2,512]{1,0:T(2,128)} %param.21) | copy-start | bytes 12292
  414.6 162.4 %copy-start.11 = (f32[2,512]{1,0:T(2,128)S(1)}, f32[2,512]{1,0:T(2,128)}, u32[]{:S(2)}) copy-start(f32[2,512]{1,0:T(2,128)} %param.20) | copy-start | bytes 12292
  414.6 204.2 %copy-start.4 = (f32[1,8,128,128]{3,2,1,0:T(8,128)S(1)}, f32[1,8,128,128]{3,2,1,0:T(8,128)}, u32[]{:S(2)}) copy-start(f32[1,8,128,128]{3,2,1,0:T(8,128)} %param.16) | copy-start | bytes 1572868
  414.7 206.9 %copy-start.5 = (f32[1,8,128,128]{3,2,1,0:T(8,128)S(1)}, f32[1,8,128,128]{3,2,1,0:T(8,128)}, u32[]{:S(2)}) copy-start(f32[1,8,128,128]{3,2,1,0:T(8,128)} %param.15) | copy-start | bytes 1572868
  414.7 206.9 %copy-start.6 = (f32[1,8,128,128]{3,2,1,0:T(8,128)S(1)}, f32[1,8,128,128]{3,2,1,0:T(8,128)}, u32[]{:S(2)}) copy-start(f32[1,8,128,128]{3,2,1,0:T(8,128)} %param.14) | copy-start | bytes 1572868
  414.7 208.6 %copy-start.3 = (f32[1,8,128,128]{3,2,1,0:T(8,128)S(1)}, f32[1,8,128,128]{3,2,1,0:T(8,128)}, u32[]{:S(2)}) copy-start(f32[1,8,128,128]{3,2,1,0:T(8,128)} %param.13) | copy-start | bytes 1572868
  414.7 204.2 %all-reduce.4.cloned.1.call-start = ((), (), s32[]{:S(2)}) async-start(), calls=%async_computation.4 | async-start | bytes 4194304
  622.4 3.0 copy-start.7
  622.4 3.0 copy-start.8
Sparse Core Ops, SparseCore 0:
  10.5 30.5 all-gather.2
  42.7 149.6 all-gather.4
  414.8 114.2 reduce-scatter.4
  531.3 87.5 all-reduce.3

commit v2 on v1

--- a/solution.py
+++ b/solution.py
@@ -72,42 +72,149 @@
     return cdf, x * e * 0.3989422804014327
 
 
-def compute_kernel(
-    tokens,
-    cotangent,
-    wg,
-    wu,
-    wo,
-    wd,
-    gains,
-    block_out,
-    input_grad,
-    gg,
-    gu,
-    go,
-    gd,
-    small,
-    n1,
-    n1t,
-    cot,
-    cott,
-    n2,
-    n2t,
-    dml,
-    dmlt,
-    forget,
-    admit,
-    cand,
-    state,
-    scan,
-    acc_a,
-    acc_b,
-    mixed,
-    act,
-    dup,
-    dpre,
-    fills,
-):
+MESH = pl.DeviceIdType.MESH
+
+
+class Exchange:
+    def __init__(self, send, recv):
+        self.send, self.recv, self.used, self.open = send, recv, 0, []
+
+    def start(self, src, dst, device):
+        k = self.used
+        self.used += 1
+        copy = pltpu.make_async_remote_copy(
+            src_ref=src,
+            dst_ref=dst,
+            send_sem=self.send.at[k],
+            recv_sem=self.recv.at[k],
+            device_id=device,
+            device_id_type=MESH,
+        )
+        copy.start()
+        self.open.append(copy)
+        return copy
+
+    def drain(self):
+        for copy in self.open:
+            copy.wait_send()
+        self.open = []
+
+
+class Gather:
+    def __init__(self, net, master, rank, slots, weights):
+        self.net, self.slots, self.weights, self.rank = net, slots, weights, rank
+        d, m = lax.axis_index("dp"), lax.axis_index("mp")
+        core, col, row = d % 2, (d // 2) % 2, d // 4
+        self.me, self.m = d, m
+        self.core = d + 1 - 2 * core
+        self.plane = [d + 2 - 4 * col, d + 4 - 8 * row, d + 6 - 4 * col - 8 * row]
+        self.order = [m, m + 1 - 2 * (m % 2), m + 2 - 4 * (m // 2), 3 - m]
+        barrier = pltpu.get_barrier_semaphore()
+        for device in [(e, m) for e in [self.core] + self.plane] + [(d, k) for k in self.order[1:]]:
+            pl.semaphore_signal(barrier, inc=1, device_id=device, device_id_type=MESH)
+        owned = master.shape[0]
+        self.owned = owned
+        for s in range(owned):
+            slots[d * owned + s] = master[s].astype(bf16)
+        pl.semaphore_wait(barrier, 7)
+
+    def rows(self, e, first, count):
+        return self.slots.at[pl.ds(e * self.owned + first, count)]
+
+    def plane_start(self):
+        n, m, (x, y, _) = self.owned, self.m, self.plane
+        h = n // 2
+        self.first = {}
+        for e, first in ((x, 0), (y, h), (x, h), (y, 0)):
+            ref = self.rows(self.me, first, h)
+            self.first[(e is y, first)] = self.net.start(ref, ref, (e, m))
+        ref = self.rows(self.me, 0, n)
+        self.sibling = [self.net.start(ref, ref, (self.core, m))]
+
+    def plane_finish(self):
+        n, m, (x, y, z) = self.owned, self.m, self.plane
+        h = n // 2
+        self.first[(False, 0)].wait_recv()
+        ref = self.rows(x, 0, h)
+        last = [self.net.start(ref, ref, (y, m))]
+        self.first[(True, h)].wait_recv()
+        ref = self.rows(y, h, h)
+        last.append(self.net.start(ref, ref, (x, m)))
+        self.first[(False, h)].wait_recv()
+        ref = self.rows(x, 0, n)
+        self.sibling.append(self.net.start(ref, ref, (self.core, m)))
+        self.first[(True, 0)].wait_recv()
+        ref = self.rows(y, 0, n)
+        self.sibling.append(self.net.start(ref, ref, (self.core, m)))
+        for copy in last:
+            copy.wait_recv()
+        ref = self.rows(z, 0, n)
+        self.sibling.append(self.net.start(ref, ref, (self.core, m)))
+        for copy in self.sibling:
+            copy.wait_recv()
+
+    def place(self, kinds):
+        wg, wu, wo, wd = self.weights
+        parts, _, hm3 = wg.shape
+        row_tiles, gates = D // BLK, hm3 // BLK
+        cols, outs = gates + wu.shape[2] // BLK, wo.shape[1] // BLK
+        for b in range(self.slots.shape[0]):
+            if b < row_tiles * cols:
+                r, c = b // cols, b % cols
+                kind, ref = (0, wg) if c < gates else (2, wu)
+                c -= 0 if c < gates else gates
+            else:
+                r, c = (b - row_tiles * cols) // row_tiles, (b - row_tiles * cols) % row_tiles
+                kind, ref = (1, wo) if r < outs else (3, wd)
+                r -= 0 if r < outs else outs
+            if kind in kinds:
+                ref[self.m, r * BLK : (r + 1) * BLK, c * BLK : (c + 1) * BLK] = self.slots[self.rank[b]]
+
+    def share(self, kind, k, e):
+        ref = self.weights[(0, 2, 1, 3)[kind]]
+        ref = (self.weights[0], self.weights[2], self.weights[1], self.weights[3])[kind]
+        size = ref.shape[1] // 8
+        return ref.at[k, pl.ds(pl.multiple_of(e * size, size), size)]
+
+    def along_start(self, kind):
+        self.along = getattr(self, "along", {})
+        for i in (1, 2, 3):
+            ref = self.share(kind, self.m, self.me)
+            self.along[kind, i] = self.net.start(ref, ref, (self.me, self.order[i]))
+
+    def spread(self, kind, i):
+        self.spreads = getattr(self, "spreads", {})
+        self.along[kind, i].wait_recv()
+        ref = self.share(kind, self.order[i], self.me)
+        self.spreads[kind, i] = (
+            [self.net.start(ref, ref, (e, self.m)) for e in self.plane],
+            [self.net.start(ref, ref, (self.core, self.m))],
+        )
+
+    def pair(self, kind, i):
+        across, inside = self.spreads[kind, i]
+        for copy, e in zip(across, self.plane):
+            copy.wait_recv()
+            ref = self.share(kind, self.order[i], e)
+            inside.append(self.net.start(ref, ref, (self.core, self.m)))
+
+    def ready(self, kind, i):
+        for copy in self.spreads[kind, i][1]:
+            copy.wait_recv()
+
+
+def compute_kernel(linked, *refs):
+    if linked:
+        tokens, cotangent, master, rank, gains = refs[:5]
+        outs = refs[5:12]
+        wg, wu, wo, wd, slots, send, recv = refs[12:19]
+        scratch = refs[19:]
+    else:
+        tokens, cotangent, wg, wu, wo, wd, gains = refs[:7]
+        outs = refs[7:14]
+        scratch = refs[14:]
+    block_out, input_grad, gg, gu, go, gd, small = outs
+    (n1, n1t, cot, cott, n2, n2t, dml, dmlt, forget, admit, cand, state, scan, acc_a, acc_b, mixed, act, dup, dpre, fills) = scratch
     parts, _, hm3 = wg.shape
     hm = hm3 // 3
     fm = wu.shape[2]
@@ -144,6 +251,14 @@
 
     half = hm // BLK
 
+    if linked:
+        net = Exchange(send, recv)
+        gather = Gather(net, master, rank, slots, (wg, wu, wo, wd))
+        gather.plane_start()
+        order = gather.order
+    else:
+        order = list(range(parts))
+
     permute_in(cotangent, cot)
     cott[...] = cot[...].T
     permute_in(tokens, n1)
@@ -158,11 +273,22 @@
 
     n1t[...] = n1[...].T
 
+    if linked:
+        gather.plane_finish()
+        gather.place((0,))
+        gather.along_start(0)
+        gather.place((1, 2, 3))
+        for kind in (1, 2, 3):
+            gather.along_start(kind)
+
     fills[0] = jnp.zeros((SUB, hm), f32)
     fills[1] = jnp.ones((SUB, hm), f32)
     weigh = fills[0]
     weigh_j = fills[0]
-    for m in range(parts):
+    for turn, m in enumerate(order):
+
+        if linked and turn:
+            gather.ready(0, turn)
 
         @pl.loop(0, L // R)
         def _(i):
@@ -171,6 +297,21 @@
             forget[m, rows, :] = dot(x, wg[m, :, :hm])
             admit[m, rows, :] = dot(x, wg[m, :, hm : 2 * hm])
             cand[m, rows, :] = dot(x, wg[m, :, 2 * hm :])
+
+        if linked and turn == 0:
+            for i in (1, 2, 3):
+                gather.spread(0, i)
+        if linked and turn == 2:
+            gather.pair(0, 3)
+        if linked and turn == 1:
+            for i in (1, 2, 3):
+                gather.spread(1, i)
+        if linked and turn == 2:
+            for kind, i in ((2, 1), (3, 1), (2, 2), (3, 2), (2, 3), (3, 3)):
+                gather.spread(kind, i)
+        if linked and turn == 3:
+            for i in (1, 2, 3):
+                gather.pair(1, i)
 
         def step(j, carry):
             s, p, k_sum, kj_sum = carry
@@ -198,20 +339,29 @@
         for _ in range(SUB - 1):
             enter = shift_down(s + p * enter)
 
+        if linked and turn == 0:
+            gather.pair(0, 1)
+        if linked and turn == 1:
+            gather.pair(0, 2)
+
         @pl.loop(0, J, unroll=4)
         def _(j):
             rows = pl.ds(pl.multiple_of(j * SUB, SUB), SUB)
             state[m, rows, :] = take(0, rows) + take(half, rows) * enter
 
-        @pl.loop(0, L // R)
-        def _(i):
-            rows = pl.ds(pl.multiple_of(i * R, R), R)
-            mixed[rows, :] += dot(state[m, rows, :].astype(bf16), wo[m])
+    if linked:
+        for i in (1, 2, 3):
+            gather.ready(1, i)
+        for kind in (2, 3):
+            gather.pair(kind, 1)
 
     @pl.loop(0, L // R)
     def _(i):
         rows = pl.ds(pl.multiple_of(i * R, R), R)
         x = mixed[rows, :]
+        for m in range(parts):
+            x += dot(state[m, rows, :].astype(bf16), wo[m])
+        mixed[rows, :] = x
         r = lax.rsqrt(jnp.mean(x * x, axis=-1, keepdims=True) + norm_eps)
         n2[rows, :] = (x * r * gain_two).astype(bf16)
         acc_a[rows, :] = x
@@ -219,7 +369,11 @@
 
     n2t[...] = n2[...].T
 
-    for m in range(parts):
+    for turn, m in enumerate(order):
+
+        if linked and turn:
+            gather.ready(2, turn)
+            gather.ready(3, turn)
 
         @pl.loop(0, L // R)
         def _(i):
@@ -234,6 +388,9 @@
             acc_a[rows, :] += dot(ac, wd[m])
             acc_b[rows, :] += dot(du, wu[m], True)
 
+        if linked and turn < 2:
+            gather.pair(2, turn + 2)
+            gather.pair(3, turn + 2)
         gd[m] = dot(cott[...], act[...]).astype(gd.dtype)
         gu[m] = dot(n2t[...], dup[...]).astype(gu.dtype)
 
@@ -256,7 +413,7 @@
     gain_sum_two = lax.fori_loop(0, L // R, back_two, gain_sum_two)
     dmlt[...] = dml[...].T
 
-    for m in range(parts):
+    for turn, m in enumerate(order):
 
         @pl.loop(0, L // R)
         def _(i):
@@ -335,16 +492,37 @@
     small[0:1, :] = gain_sum_one
     small[1:2, :] = gain_sum_two
     small[2:3, :hm] = jnp.sum(weigh, axis=0, keepdims=True)
+    if linked:
+        net.drain()
     small[3:4, :hm] = jnp.sum(weigh_j + weigh * place, axis=0, keepdims=True)
 
 
-def compute(tokens, cotangent, wg, wu, wo, wd, gains, grad_type):
-    parts, _, hm3 = wg.shape
-    hm, fm = hm3 // 3, wu.shape[2]
+def compute(tokens, cotangent, gains, grad_type, weights=None, master=None, rank=None):
+    linked = weights is None
+    parts = lax.axis_size("mp")
+    hm, fm = H // parts, FF // parts
     sds = jax.ShapeDtypeStruct
     vm = pl.BlockSpec(memory_space=pltpu.VMEM)
+    if linked:
+        args = (tokens, cotangent, master, rank, gains)
+        in_specs = [vm, vm, vm, pl.BlockSpec(memory_space=pltpu.SMEM), vm]
+        extra = [
+            pltpu.VMEM((parts, D, 3 * hm), bf16),
+            pltpu.VMEM((parts, D, fm), bf16),
+            pltpu.VMEM((parts, hm, D), bf16),
+            pltpu.VMEM((parts, fm, D), bf16),
+            pltpu.VMEM((rank.shape[0], BLK, BLK), bf16),
+            pltpu.SemaphoreType.DMA((128,)),
+            pltpu.SemaphoreType.DMA((128,)),
+        ]
+        params = dict(collective_id=0, has_side_effects=True)
+    else:
+        args = (tokens, cotangent, *weights, gains)
+        in_specs = [vm] * 7
+        extra = []
+        params = {}
     return pl.pallas_call(
-        compute_kernel,
+        functools.partial(compute_kernel, linked),
         out_shape=(
             sds((L, D), bf16),
             sds((L, D), f32),
@@ -354,9 +532,9 @@
             sds((parts, D, fm), grad_type),
             sds((8, D), f32),
         ),
-        in_specs=[vm] * 7,
+        in_specs=in_specs,
         out_specs=[vm] * 7,
-        scratch_shapes=[
+        scratch_shapes=extra + [
             pltpu.VMEM((L, D), bf16),
             pltpu.VMEM((D, L), bf16),
             pltpu.VMEM((L, D), bf16),
@@ -378,9 +556,9 @@
             pltpu.VMEM((L, 3 * hm), bf16),
             pltpu.VMEM((2, SUB, hm), f32),
         ],
-        compiler_params=pltpu.CompilerParams(vmem_limit_bytes=63 * 2**20),
+        compiler_params=pltpu.CompilerParams(vmem_limit_bytes=63 * 2**20, **params),
         name="block",
-    )(tokens, cotangent, wg, wu, wo, wd, gains)
+    )(*args)
 
 
 def adam_update(first_old, second_old, gradient):
@@ -419,18 +597,23 @@
     hm, fm = H // parts, FF // parts
     token_total = L * data_parts * parts
     row_tiles, cols, lows = D // BLK, (3 * hm + fm) // BLK, (hm + fm) // BLK
-    slot_order = jnp.argsort(owner, stable=True)
-    block_rank = jnp.argsort(slot_order, stable=True)
-    stored = lax.all_gather(master.astype(bf16), "dp", axis=1, tiled=True)
-    stored = lax.all_gather(stored, "mp", axis=0, tiled=True)
-    stack = stored[:, block_rank]
-    upper = stack[:, : row_tiles * cols].reshape(parts, row_tiles, cols, BLK, BLK)
-    upper = upper.transpose(0, 1, 3, 2, 4).reshape(parts, D, cols * BLK)
-    lower = stack[:, row_tiles * cols :].reshape(parts, lows, row_tiles, BLK, BLK)
-    lower = lower.transpose(0, 1, 3, 2, 4).reshape(parts, lows * BLK, D)
-    block_out, input_grad, gg, gu, go, gd, small = compute(
-        tokens, cotangent, upper[:, :, : 3 * hm], upper[:, :, 3 * hm :], lower[:, :hm], lower[:, hm:], gains, bf16
-    )
+    number = jnp.arange(owner.shape[0], dtype=jnp.int32)
+    ahead = (owner[None, :] < owner[:, None]) | ((owner[None, :] == owner[:, None]) & (number[None, :] < number[:, None]))
+    block_rank = jnp.sum(ahead.astype(jnp.int32), axis=1)
+    slot_order = jnp.sum(jnp.where(block_rank[None, :] == number[:, None], number[None, :], 0), axis=1)
+    if data_parts == 8 and parts == 4:
+        outs = compute(tokens, cotangent, gains, bf16, master=master[0], rank=block_rank)
+    else:
+        stored = lax.all_gather(master.astype(bf16), "dp", axis=1, tiled=True)
+        stored = lax.all_gather(stored, "mp", axis=0, tiled=True)
+        stack = stored[:, block_rank]
+        upper = stack[:, : row_tiles * cols].reshape(parts, row_tiles, cols, BLK, BLK)
+        upper = upper.transpose(0, 1, 3, 2, 4).reshape(parts, D, cols * BLK)
+        lower = stack[:, row_tiles * cols :].reshape(parts, lows, row_tiles, BLK, BLK)
+        lower = lower.transpose(0, 1, 3, 2, 4).reshape(parts, lows * BLK, D)
+        weights = (upper[:, :, : 3 * hm], upper[:, :, 3 * hm :], lower[:, :hm], lower[:, hm:])
+        outs = compute(tokens, cotangent, gains, bf16, weights=weights)
+    block_out, input_grad, gg, gu, go, gd, small = outs
     upper = jnp.concatenate([gg, gu], axis=2).reshape(parts, row_tiles, BLK, cols, BLK).transpose(0, 1, 3, 2, 4)
     upper = upper.reshape(parts, row_tiles * cols, BLK, BLK)
     lower = jnp.concatenate([go, gd], axis=2).reshape(parts, row_tiles, BLK, lows, BLK).transpose(0, 3, 1, 4, 2)

time: 635 us -> 417 us (0.66)
  waiting for transfers between devices: 334 us -> 157 us
  local copies, waits for them, and re-layouts: 118 us -> 58.8 us
  Pallas kernels: 88.5 us -> 112 us
    all_gather x2 -> x0, waiting for transfers between devices: 178 us -> none  [the longest x1 146 us: on_device(): stored = lax.all_gather(stored, 'mp', axis=0, tiled=True)]
    reshape x4 -> x0, local copies, waits for them, and re-layouts: 28 us -> none  [the longest x1 8.99 us: on_device(): stack[:, :row_tiles * cols].reshape(parts, row_tiles, cols, BLK, BLK)]
    pallas_call x1, Pallas kernels: 88.5 us -> 112 us  [compute(): pl.pallas_call(functools.partial(compute_kernel, linked), out_shape=(sds(...]
    slice x7 -> x0, local copies, waits for them, and re-layouts: 18.4 us -> none  [the longest x1 6.9 us: on_device(): stack[:, :row_tiles * cols].reshape(parts, row_tiles, cols, BLK, BLK)]
    gather x1 -> x0, local copies, waits for them, and re-layouts: 8.92 us -> none  [on_device(): stack = stored[:, block_rank]]
    unnamed x5 -> x3, waiting for transfers between devices: 41.3 us -> 41.2 us
  transfers between devices with their start and end apart: 4 -> 2, of which waited for: 4 -> 2; matrix products, arithmetic and copies ran while one was open for 1% -> 1% of each run, Pallas kernels for 0% -> 0%
where the time goes in v2:
time: 417 us; the launch traced here: 416 us
  waiting for transfers between devices  157 us (38%)
  Pallas kernels  112 us (27%)
  local copies, waits for them, and re-layouts  58.8 us (14%)
  blocking collectives  43.3 us (10%)
  other arithmetic  19.7 us (5%)
  between operations  17.3 us (4%)
  matrix products  7.63 us (2%)
    reduce_scatter x1, waiting for transfers between devices, on_device(): lax.psum_scatter(natural[:, slot_order], 'dp', scatter_dimension=1, tiled...  115 us
    pallas_call x1, Pallas kernels, compute(): pl.pallas_call(functools.partial(compute_kernel, linked), out_shape=(sds(...  112 us
    psum x1, blocking collectives, on_device(): gain_grad, forget_total = lax.psum((small[:2], forget_part), ('dp', 'mp'))  43.3 us
    unnamed x3, waiting for transfers between devices  41.2 us
    gather x1, local copies, waits for them, and re-layouts, on_device(): natural[:, slot_order]  14.6 us
    convert_element_type x1, other arithmetic, on_device(): natural = jnp.concatenate([upper, lower], axis=1).astype(f32)  10.3 us
    transpose x1, local copies, waits for them, and re-layouts, on_device(): jnp.concatenate([gg, gu], axis=2).reshape(parts, row_tiles, BLK, cols, BLK)  8.9 us
  transfers between devices with their start and end apart: 2, of which 2 were waited for; matrix products, arithmetic and copies ran while one was open for 1% of the time, Pallas kernels for 0%

profile of v2, /device:TPU:0, one launch (start us, length us, event | category | flops | bytes accessed | tf_op | source)
XLA Modules:
  0.0 415.5 jit_solution(13905703305176075241)
XLA Ops:
  7.2 0.0 copy-start
  7.2 0.0 reduce-scatter.5.cloned.1.call-start
  7.2 0.9 convert_reduce_fusion.refs_3_
  8.2 0.0 copy-start.13
  8.2 0.1 select_reduce_fusion
  8.3 0.4 copy-done.13
  8.7 112.1 %block.1 = (bf16[1024,512]{1,0:T(8,128)(2,1)}, f32[1024,512]{1,0:T(8,128)}, bf16[4,512,768]{2,1,0:T(8,128)(2,1)}, bf16[4,512,512]{2,1,0:T(8,128)(2,1)}, bf16[4,5...) custom-call(bf16[1024,512]{1,0:T(8,128)(2,1)} %refs_0_.1, bf16[1024,512]{1,0:T(8,128)(2,1)} %refs_1_.1, ...), custom_call_target="tpu_custom_call" | custom-call | tf_op jit(solution)/shard_map/block/pallas_call | solution.py:524
  120.8 3.7 pad_maximum_fusion.1
  124.5 4.7 %copy.35 = bf16[4,512,768]{1,2,0:T(8,128)(2,1)} copy(bf16[4,512,768]{2,1,0:T(8,128)(2,1)} %pad_maximum_fusion.1) | data formatting | bytes 6291456 | tf_op jit(solution)/shard_map/concatenate | solution.py:619
  129.3 0.0 copy-start.2
  129.3 5.6 %reshape.74 = bf16[4,4,128,6,128]{2,1,4,3,0:T(4,128)(2,1)} reshape(bf16[4,512,768]{1,2,0:T(8,128)(2,1)} %copy.35) | data formatting | bytes 6291456 | tf_op jit(solution)/shard_map/reshape | solution.py:619
  134.9 0.0 copy-start.1
  134.9 4.6 %copy.36 = bf16[4,6,4,128,128]{4,3,2,1,0:T(8,128)(2,1)} copy(bf16[4,6,4,128,128]{4,2,3,1,0:T(4,128)(2,1)} %bitcast.63) | data formatting | bytes 6291456 | tf_op jit(solution)/shard_map/transpose | solution.py:619
  139.5 0.0 copy-done.2
  139.5 0.0 copy-done.1
  139.5 2.7 pad_maximum_fusion
  142.2 7.9 %copy.33 = bf16[4,512,1280]{1,2,0:T(8,128)(2,1)} copy(bf16[4,512,1280]{2,1,0:T(8,128)(2,1)} %pad_maximum_fusion) | data formatting | bytes 10485760 | tf_op jit(solution)/shard_map/concatenate | solution.py:617
  150.0 8.3 %reshape.72 = bf16[4,4,128,10,128]{2,1,4,3,0:T(4,128)(2,1)} reshape(bf16[4,512,1280]{1,2,0:T(8,128)(2,1)} %copy.33) | data formatting | bytes 10485760 | tf_op jit(solution)/shard_map/reshape | solution.py:617
  158.3 8.9 %copy.34 = bf16[4,4,10,128,128]{4,3,2,1,0:T(8,128)(2,1)} copy(bf16[4,4,10,128,128]{3,1,4,2,0:T(4,128)(2,1)} %bitcast.60) | data formatting | bytes 10485760 | tf_op jit(solution)/shard_map/transpose | solution.py:617
  167.2 10.3 %maximum_convert_fusion = f32[4,64,128,128]{3,2,1,0:T(8,128)} fusion(bf16[4,24,128,128]{3,2,1,0:T(8,128)(2,1)} %bitcast.62, bf16[4,40,128,128]{3,2,1,0:T(8,128)(2,1)} %bitcast.61), kind=kLoop, calls=%fused_computation.1 | loop fusion | flops 8388608 | bytes 25165824 | tf_op jit(solution)/shard_map/convert_element_type | solution.py:621
  177.5 14.6 %gather_fusion = f32[64,4,128,128]{3,2,1,0:T(8,128)} fusion(f32[4,64,128,128]{3,2,1,0:T(8,128)} %maximum_convert_fusion, s32[1024]{0:T(1024)S(1)} %pad_clamp_fusion), kind=kCustom, calls=%fused_computation | custom fusion | bytes 33554688 | tf_op jit(solution)/shard_map/gather | solution.py:622
  192.1 0.0 copy-start.14
  192.1 0.0 copy-start.10
  192.1 0.0 copy-start.11
  192.1 0.0 copy-start.12
  192.1 0.0 copy-start.6
  192.1 0.0 copy-start.7
  192.2 0.0 reduce-scatter.5.cloned.1.call-update
  192.2 0.0 copy-start.4
  192.2 0.0 all-reduce.4.cloned.1.call-start
  192.2 115.4 %reduce-scatter.5.cloned.1.call-done = f32[4,8,128,128]{3,2,0,1:T(8,128)} async-done(((f32[4,64,128,128]{3,2,0,1:T(8,128)}), f32[4,8,128,128]{3,2,0,1:T(8,128)}) %reduce-scatter.5.cloned.1.call-update) | async-done | bytes 2097168 | tf_op jit(solution)/shard_map/reduce_scatter | solution.py:622
  307.6 0.0 all-reduce.4.cloned.1.call-update
  307.6 0.0 copy-start.5
  307.6 0.8 slice.9
  308.5 0.0 copy-done.14
  308.5 0.6 dynamic-slice
  309.0 1.4 slice_reduce_fusion
  311.7 43.3 %all-reduce.1 = (f32[2,512]{1,0:T(2,128)S(1)}, f32[]{:T(128)}) all-reduce(f32[2,512]{1,0:T(2,128)S(1)} %slice.9, f32[]{:T(128)S(6)} %div.30), channel_id=1, replica_groups=mesh['dp'=8,'mp'=4] {'dp','mp'}, use_global_device_ids=true, to_apply=%region_4.5 | all-reduce | flops 1025 | bytes 8200 | tf_op jit(solution)/shard_map/psum | solution.py:627
  355.7 0.0 copy-done.10
  355.7 0.0 copy-done.11
  355.7 0.0 copy-done.12
  355.7 0.6 multiply_subtract_fusion
  356.3 41.2 %all-reduce.4.cloned.1.call-done = f32[4,8,128,128]{3,2,0,1:T(8,128)} async-done(((f32[4,8,128,128]{3,2,0,1:T(8,128)}), f32[4,8,128,128]{3,2,0,1:T(8,128)}) %all-reduce.4.cloned.1.call-update) | async-done | bytes 2097168
  397.5 0.0 copy-done.6
  397.5 2.7 fusion.6
  400.2 0.0 copy-done
  400.2 0.0 copy-done.7
  400.2 0.0 copy-start.3
  400.2 1.9 fusion.5
  402.2 0.0 copy-start.8
  402.2 0.0 copy-start.9
  402.2 0.9 fusion.7
  403.1 0.0 copy-done.4
  403.1 2.1 fusion.29
  405.2 0.0 copy-done.5
  405.2 1.0 copy.50
  406.2 0.0 copy-done.3
  406.2 1.3 copy.51
  407.5 0.0 copy-done.8
  407.5 0.0 copy-done.9
  (2 shorter events, 0.0 us)
Async XLA Ops:
  7.2 393.0 %copy-start = (f32[1,8,128,128]{3,2,1,0:T(8,128)S(1)}, f32[1,8,128,128]{3,2,1,0:T(8,128)}, u32[]{:S(2)}) copy-start(f32[1,8,128,128]{3,2,1,0:T(8,128)} %param.17) | copy-start | bytes 1572868
  7.2 300.4 %reduce-scatter.5.cloned.1.call-start = ((), (), s32[]{:S(2)}) async-start(), calls=%async_computation.1 | async-start | bytes 18874368 | tf_op jit(solution)/shard_map/reduce_scatter | solution.py:622
  8.2 0.5 copy-start.13
  129.3 10.2 %copy-start.2 = (bf16[4,512,512]{2,1,0:T(8,128)(2,1)S(1)}, bf16[4,512,512]{2,1,0:T(8,128)(2,1)}, u32[]{:S(2)}) copy-start(bf16[4,512,512]{2,1,0:T(8,128)(2,1)} %get-tuple-element.20) | copy-start | bytes 6291460
  134.9 4.6 %copy-start.1 = (bf16[4,512,768]{2,1,0:T(8,128)(2,1)S(1)}, bf16[4,512,768]{2,1,0:T(8,128)(2,1)}, u32[]{:S(2)}) copy-start(bf16[4,512,768]{2,1,0:T(8,128)(2,1)} %get-tuple-element.19) | copy-start | bytes 9437188
  192.1 116.3 %copy-start.14 = (u32[32]{0:T(128)S(1)}, u32[32]{0:T(128)}, u32[]{:S(2)}) copy-start(u32[32]{0:T(128)} %constant.53) | copy-start | bytes 388
  192.1 163.6 %copy-start.10 = (f32[2,512]{1,0:T(2,128)S(1)}, f32[2,512]{1,0:T(2,128)}, u32[]{:S(2)}) copy-start(f32[2,512]{1,0:T(2,128)} %refs_4_.1) | copy-start | bytes 12292
  192.1 163.6 %copy-start.11 = (f32[2,512]{1,0:T(2,128)S(1)}, f32[2,512]{1,0:T(2,128)}, u32[]{:S(2)}) copy-start(f32[2,512]{1,0:T(2,128)} %param.21) | copy-start | bytes 12292
  192.1 163.6 %copy-start.12 = (f32[2,512]{1,0:T(2,128)S(1)}, f32[2,512]{1,0:T(2,128)}, u32[]{:S(2)}) copy-start(f32[2,512]{1,0:T(2,128)} %param.20) | copy-start | bytes 12292
  192.1 205.4 %copy-start.6 = (f32[1,8,128,128]{3,2,1,0:T(8,128)S(1)}, f32[1,8,128,128]{3,2,1,0:T(8,128)}, u32[]{:S(2)}) copy-start(f32[1,8,128,128]{3,2,1,0:T(8,128)} %param.16) | copy-start | bytes 1572868
  192.1 208.1 %copy-start.7 = (f32[1,8,128,128]{3,2,1,0:T(8,128)S(1)}, f32[1,8,128,128]{3,2,1,0:T(8,128)}, u32[]{:S(2)}) copy-start(f32[1,8,128,128]{3,2,1,0:T(8,128)} %param.15) | copy-start | bytes 1572868
  192.2 210.9 %copy-start.4 = (f32[1,8,128,128]{3,2,1,0:T(8,128)S(1)}, f32[1,8,128,128]{3,2,1,0:T(8,128)}, u32[]{:S(2)}) copy-start(f32[1,8,128,128]{3,2,1,0:T(8,128)} %param.13) | copy-start | bytes 1572868
  192.2 205.3 %all-reduce.4.cloned.1.call-start = ((), (), s32[]{:S(2)}) async-start(), calls=%async_computation.2 | async-start | bytes 4194304
  307.6 97.6 %copy-start.5 = (bf16[1024,512]{1,0:T(8,128)(2,1)S(1)}, bf16[1024,512]{1,0:T(8,128)(2,1)}, u32[]{:S(2)}) copy-start(bf16[1024,512]{1,0:T(8,128)(2,1)} %get-tuple-element.45) | copy-start | bytes 3145732
  400.2 6.0 %copy-start.3 = (f32[1024,512]{1,0:T(8,128)S(1)}, f32[1024,512]{1,0:T(8,128)}, u32[]{:S(2)}) copy-start(f32[1024,512]{1,0:T(8,128)} %get-tuple-element.46) | copy-start | bytes 6291460
  402.2 5.3 %copy-start.8 = (f32[1,8,128,128]{3,2,1,0:T(8,128)}, f32[1,8,128,128]{3,2,1,0:T(8,128)S(1)}, u32[]{:S(2)}) copy-start(f32[1,8,128,128]{3,2,1,0:T(8,128)S(1)} %get-tuple-element.48) | copy-start | bytes 1572868
  402.2 5.3 %copy-start.9 = (f32[1,8,128,128]{3,2,1,0:T(8,128)}, f32[1,8,128,128]{3,2,1,0:T(8,128)S(1)}, u32[]{:S(2)}) copy-start(f32[1,8,128,128]{3,2,1,0:T(8,128)S(1)} %get-tuple-element.47) | copy-start | bytes 1572868
Sparse Core Ops, SparseCore 0:
  192.3 115.2 reduce-scatter.4
  310.0 87.5 all-reduce.3

commit v3 on v2

--- a/solution.py
+++ b/solution.py
@@ -105,7 +105,7 @@
         self.net, self.slots, self.weights, self.rank = net, slots, weights, rank
         d, m = lax.axis_index("dp"), lax.axis_index("mp")
         core, col, row = d % 2, (d // 2) % 2, d // 4
-        self.me, self.m = d, m
+        self.me, self.m, self.side = d, m, core
         self.core = d + 1 - 2 * core
         self.plane = [d + 2 - 4 * col, d + 4 - 8 * row, d + 6 - 4 * col - 8 * row]
         self.order = [m, m + 1 - 2 * (m % 2), m + 2 - 4 * (m // 2), 3 - m]
@@ -154,7 +154,7 @@
             copy.wait_recv()
 
     def place(self, kinds):
-        wg, wu, wo, wd = self.weights
+        wg, wo, wu, wd = self.weights
         parts, _, hm3 = wg.shape
         row_tiles, gates = D // BLK, hm3 // BLK
         cols, outs = gates + wu.shape[2] // BLK, wo.shape[1] // BLK
@@ -171,8 +171,7 @@
                 ref[self.m, r * BLK : (r + 1) * BLK, c * BLK : (c + 1) * BLK] = self.slots[self.rank[b]]
 
     def share(self, kind, k, e):
-        ref = self.weights[(0, 2, 1, 3)[kind]]
-        ref = (self.weights[0], self.weights[2], self.weights[1], self.weights[3])[kind]
+        ref = self.weights[kind]
         size = ref.shape[1] // 8
         return ref.at[k, pl.ds(pl.multiple_of(e * size, size), size)]
 
@@ -203,23 +202,156 @@
             copy.wait_recv()
 
 
+class Reduce:
+    def __init__(self, net, gather, grads, spans, inside, across, along):
+        self.net, self.g, self.grads, self.spans = net, gather, grads, spans
+        self.inside, self.across, self.along = inside, across, along
+        self.size = grads.shape[1] // 8
+        self.copies = {}
+
+    def place(self, e):
+        return (e % 2) * 4 + e // 2
+
+    def rows(self, first, count):
+        return pl.ds(pl.multiple_of(first * self.size, self.size), count * self.size)
+
+    def chip(self, kind, i):
+        g, cols = self.g, self.spans[kind]
+        src = self.grads.at[g.order[i], self.rows((1 - g.side) * 4, 4), cols]
+        dst = self.inside.at[i - 1, :, cols]
+        self.copies[0, kind, i] = self.net.start(src, dst, (g.core, g.m))
+
+    def plane(self, kind, i):
+        g, cols = self.g, self.spans[kind]
+        self.copies[0, kind, i].wait_recv()
+        m = g.order[i]
+        rows = self.rows(g.side * 4, 4)
+        total = self.grads[m, rows, cols].astype(f32) + self.inside[i - 1, :, cols].astype(f32)
+        self.grads[m, rows, cols] = total.astype(bf16)
+        for k, e in enumerate(g.plane):
+            src = self.grads.at[m, self.rows(self.place(e), 1), cols]
+            self.copies[1, kind, i, k] = self.net.start(src, self.across.at[i - 1, k, :, cols], (e, g.m))
+
+    def model(self, kind, i):
+        g, cols = self.g, self.spans[kind]
+        m = g.order[i]
+        rows = self.rows(self.place(g.me), 1)
+        total = self.grads[m, rows, cols].astype(f32)
+        for k in range(3):
+            self.copies[1, kind, i, k].wait_recv()
+            total += self.across[i - 1, k, :, cols].astype(f32)
+        self.grads[m, rows, cols] = total.astype(bf16)
+        src = self.grads.at[m, rows, cols]
+        self.copies[2, kind, i] = self.net.start(src, self.along.at[i - 1, :, cols], (g.me, m))
+
+    def own(self, kind):
+        g, cols = self.g, self.spans[kind]
+        rows = self.rows(self.place(g.me), 1)
+        total = self.grads[g.m, rows, cols].astype(f32)
+        for i in (1, 2, 3):
+            self.copies[2, kind, i].wait_recv()
+            total += self.along[i - 1, :, cols].astype(f32)
+        self.grads[g.m, rows, cols] = total.astype(bf16)
+
+    def into_slots(self, stack, out, slot_order):
+        g = self.g
+        row_tiles = D // BLK
+        gate, outs, ups, downs = self.spans
+        cols = (gate.stop - gate.start + ups.stop - ups.start) // BLK
+        gates, lows = gate.stop // BLK, (outs.stop - outs.start) // BLK
+        for b in range(stack.shape[0]):
+            if b < row_tiles * cols:
+                r, c = b // cols, b % cols
+                first = c * BLK if c < gates else ups.start + (c - gates) * BLK
+            else:
+                k, r = (b - row_tiles * cols) // row_tiles, (b - row_tiles * cols) % row_tiles
+                first = outs.start + k * BLK if k < lows else downs.start + (k - lows) * BLK
+            stack[b] = self.grads[g.m, r * BLK : (r + 1) * BLK, first : first + BLK]
+        n = stack.shape[0] // 8
+        for s in range(stack.shape[0]):
+            out[self.place(s // n) * n + s % n] = stack[slot_order[s]]
+
+    def slots_chip(self, out, pair):
+        g, n = self.g, out.shape[0] // 8
+        self.last = []
+        for e in (g.plane[2], g.plane[0], g.plane[1], g.me):
+            src = out.at[pl.ds(((1 - g.side) * 4 + e // 2) * n, n)]
+            self.last.append(self.net.start(src, pair.at[pl.ds((e // 2) * n, n)], (g.core, g.m)))
+
+    def slots_plane(self, out, pair, far):
+        g, n = self.g, out.shape[0] // 8
+        self.ends = []
+        for copy, e, k in zip(self.last, (g.plane[2], g.plane[0], g.plane[1]), (2, 0, 1)):
+            copy.wait_recv()
+            rows = pl.ds((g.side * 4 + e // 2) * n, n)
+            out[rows] = (out[rows].astype(f32) + pair[pl.ds((e // 2) * n, n)].astype(f32)).astype(bf16)
+            self.ends.append(self.net.start(out.at[rows], far.at[k], (e, g.m)))
+        self.last[3].wait_recv()
+
+    def slots_end(self, out, pair, far, owned):
+        g, n = self.g, out.shape[0] // 8
+        total = out[pl.ds((g.side * 4 + g.me // 2) * n, n)].astype(f32)
+        total += pair[pl.ds((g.me // 2) * n, n)].astype(f32)
+        for copy in self.ends:
+            copy.wait_recv()
+        for k in range(3):
+            total += far[k].astype(f32)
+        owned[...] = total
+
+
+class SmallSum:
+    def __init__(self, net, gather, values, along, across, inside):
+        self.net, self.g, self.values = net, gather, values
+        self.slots = (along, across, inside)
+        self.peers = (
+            [(gather.me, k) for k in gather.order[1:]],
+            [(e, gather.m) for e in gather.plane],
+            [(gather.core, gather.m)],
+        )
+        self.mine = (gather.m, gather.me // 2, gather.side)
+        self.open = []
+
+    def send(self, stage):
+        slot = self.slots[stage]
+        slot[self.mine[stage]] = self.values[...]
+        ref = slot.at[self.mine[stage]]
+        self.open = [self.net.start(ref, ref, peer) for peer in self.peers[stage]]
+
+    def add(self, stage):
+        for copy in self.open:
+            copy.wait_recv()
+        slot = self.slots[stage]
+        total = slot[0]
+        for k in range(1, slot.shape[0]):
+            total += slot[k]
+        self.values[...] = total
+
+
 def compute_kernel(linked, *refs):
     if linked:
-        tokens, cotangent, master, rank, gains = refs[:5]
-        outs = refs[5:12]
-        wg, wu, wo, wd, slots, send, recv = refs[12:19]
-        scratch = refs[19:]
+        tokens, cotangent, master, rank, slot_order, gains = refs[:6]
+        block_out, input_grad, owned, small = refs[6:10]
+        wg, wo, wu, wd, grads, slots, turned, pair, far, inside, across, along, sum_a, sum_b, sum_c, send, recv = refs[10:27]
+        scratch = refs[27:]
     else:
-        tokens, cotangent, wg, wu, wo, wd, gains = refs[:7]
-        outs = refs[7:14]
-        scratch = refs[14:]
-    block_out, input_grad, gg, gu, go, gd, small = outs
-    (n1, n1t, cot, cott, n2, n2t, dml, dmlt, forget, admit, cand, state, scan, acc_a, acc_b, mixed, act, dup, dpre, fills) = scratch
+        tokens, cotangent, base, wg, wo, wu, wd, gains = refs[:8]
+        block_out, input_grad, grads, small = refs[8:12]
+        scratch = refs[12:]
+    (n1, n1t, cot, cott, n2, n2t, forget, admit, cand, state, scan, acc_a, acc_b, mixed, mid, fills, local) = scratch
+    dml, dmlt = n2, n2t
     parts, _, hm3 = wg.shape
     hm = hm3 // 3
     fm = wu.shape[2]
+    spans = (slice(0, 3 * hm), slice(3 * hm, 4 * hm), slice(4 * hm, 4 * hm + fm), slice(4 * hm + fm, 4 * hm + 2 * fm))
+    gate, outs, ups, downs = spans
+    act, dup, dpre = mid.at[:, :fm], mid.at[:, fm:], mid.at[:, : 3 * hm]
     gain_one = gains[0:1, :]
     gain_two = gains[1:2, :]
+
+    fetch_cot = pltpu.make_async_copy(cotangent, cot, local.at[0])
+    fetch_tok = pltpu.make_async_copy(tokens, n1, local.at[1])
+    fetch_cot.start()
+    fetch_tok.start()
 
     def permute_in(src, dst):
         for k in range(D // BLK):
@@ -253,15 +385,18 @@
 
     if linked:
         net = Exchange(send, recv)
-        gather = Gather(net, master, rank, slots, (wg, wu, wo, wd))
+        gather = Gather(net, master, rank, slots, (wg, wo, wu, wd))
         gather.plane_start()
+        reduce = Reduce(net, gather, grads, spans, inside, across, along)
         order = gather.order
     else:
         order = list(range(parts))
 
-    permute_in(cotangent, cot)
+    fetch_cot.wait()
+    permute_in(cot, cot)
     cott[...] = cot[...].T
-    permute_in(tokens, n1)
+    fetch_tok.wait()
+    permute_in(n1, n1)
     mixed[...] = n1[...].astype(f32)
 
     @pl.loop(0, L // R)
@@ -391,10 +526,26 @@
         if linked and turn < 2:
             gather.pair(2, turn + 2)
             gather.pair(3, turn + 2)
-        gd[m] = dot(cott[...], act[...]).astype(gd.dtype)
-        gu[m] = dot(n2t[...], dup[...]).astype(gu.dtype)
-
-    permute_out(acc_a, block_out)
+        if linked and turn >= 2:
+            reduce.plane(2, turn - 1)
+            reduce.plane(3, turn - 1)
+        if linked and turn == 3:
+            reduce.model(2, 1)
+            reduce.model(3, 1)
+        grads[m, :, downs] = dot(cott[...], act[...]).astype(bf16)
+        grads[m, :, ups] = dot(n2t[...], dup[...]).astype(bf16)
+        if linked and turn:
+            reduce.chip(2, turn)
+            reduce.chip(3, turn)
+
+    permute_out(acc_a, n1)
+    push_out = pltpu.make_async_copy(n1, block_out, local.at[0])
+    push_out.start()
+
+    if linked:
+        for kind in (2, 3):
+            reduce.plane(kind, 3)
+            reduce.model(kind, 2)
 
     gain_sum_two = jnp.zeros((1, D), f32)
 
@@ -412,8 +563,10 @@
 
     gain_sum_two = lax.fori_loop(0, L // R, back_two, gain_sum_two)
     dmlt[...] = dml[...].T
-
-    for turn, m in enumerate(order):
+    fetch_tok = pltpu.make_async_copy(tokens, cot, local.at[1])
+    fetch_tok.start()
+
+    for turn, m in reversed(list(enumerate(order))):
 
         @pl.loop(0, L // R)
         def _(i):
@@ -464,19 +617,42 @@
         last = state[m, pl.ds(L - SUB, SUB), :]
         lax.fori_loop(0, J // 2, back, shift_down(last), unroll=2)
 
-        gg[m] = dot(n1t[...], dpre[...]).astype(gg.dtype)
-        go[m] = dot(dmlt[...], state[m].astype(bf16)).astype(go.dtype)
+        if linked:
+            if turn == 3:
+                for kind in (2, 3):
+                    reduce.model(kind, 3)
+            if turn == 1:
+                for kind in (0, 1):
+                    reduce.model(kind, 3)
+            if turn == 0:
+                for kind in (0, 1):
+                    reduce.model(kind, 2)
+            if turn < 3:
+                for kind in (0, 1):
+                    reduce.plane(kind, turn + 1)
+        grads[m, :, gate] = dot(n1t[...], dpre[...]).astype(bf16)
+        grads[m, :, outs] = dot(dmlt[...], state[m].astype(bf16)).astype(bf16)
+        if linked and turn:
+            for kind in (0, 1):
+                reduce.chip(kind, turn)
 
         @pl.loop(0, L // R)
         def _(i):
             rows = pl.ds(pl.multiple_of(i * R, R), R)
             acc_b[rows, :] += dot(dpre[rows, :], wg[m], True)
 
-    permute_in(tokens, n1)
+    fetch_tok.wait()
+    permute_in(cot, cot)
+
+    if linked:
+        for kind in (0, 1):
+            reduce.model(kind, 1)
+        for kind in (2, 3):
+            reduce.own(kind)
 
     def back_one(i, total):
         rows = pl.ds(pl.multiple_of(i * R, R), R)
-        x = n1[rows, :].astype(f32)
+        x = cot[rows, :].astype(f32)
         r = lax.rsqrt(jnp.mean(x * x, axis=-1, keepdims=True) + norm_eps)
         dn = acc_b[rows, :]
         q = dn * gain_one
@@ -485,78 +661,99 @@
 
     gain_sum_one = lax.fori_loop(0, L // R, back_one, jnp.zeros((1, D), f32))
 
-    permute_out(mixed, input_grad)
-
     place = lax.broadcasted_iota(jnp.int32, (SUB, hm), 0).astype(f32) * float(J)
+    if linked:
+        first = ((gather.me * parts + gather.m) * L + 1).astype(f32)
+        token_total = float(L * parts * lax.axis_size("dp"))
+    else:
+        first = base[0]
+        token_total = base[1]
+    forget_sum = jnp.sum(weigh_j + weigh * (place + first), axis=0, keepdims=True) / token_total
     small[...] = jnp.zeros_like(small)
     small[0:1, :] = gain_sum_one
     small[1:2, :] = gain_sum_two
-    small[2:3, :hm] = jnp.sum(weigh, axis=0, keepdims=True)
+    small[2:3, :hm] = forget_sum
+
     if linked:
+        tiny = SmallSum(net, gather, small, sum_a, sum_b, sum_c)
+        tiny.send(0)
+        for kind in (0, 1):
+            reduce.own(kind)
         net.drain()
-    small[3:4, :hm] = jnp.sum(weigh_j + weigh * place, axis=0, keepdims=True)
-
-
-def compute(tokens, cotangent, gains, grad_type, weights=None, master=None, rank=None):
+        reduce.into_slots(slots, turned, slot_order)
+        reduce.slots_chip(turned, pair)
+        tiny.add(0)
+        tiny.send(1)
+        reduce.slots_plane(turned, pair, far)
+
+    permute_out(mixed, acc_a)
+    push_grad = pltpu.make_async_copy(acc_a, input_grad, local.at[2])
+    push_grad.start()
+
+    if linked:
+        tiny.add(1)
+        tiny.send(2)
+        reduce.slots_end(turned, pair, far, owned)
+        tiny.add(2)
+        net.drain()
+    push_out.wait()
+    push_grad.wait()
+
+
+def compute(tokens, cotangent, gains, weights=None, base=None, master=None, rank=None, slot_order=None):
     linked = weights is None
     parts = lax.axis_size("mp")
     hm, fm = H // parts, FF // parts
+    wide = 4 * hm + 2 * fm
     sds = jax.ShapeDtypeStruct
-    vm = pl.BlockSpec(memory_space=pltpu.VMEM)
+    vm, sm, hbm = (pl.BlockSpec(memory_space=k) for k in (pltpu.VMEM, pltpu.SMEM, pl.ANY))
     if linked:
-        args = (tokens, cotangent, master, rank, gains)
-        in_specs = [vm, vm, vm, pl.BlockSpec(memory_space=pltpu.SMEM), vm]
+        n = rank.shape[0]
+        args = (tokens, cotangent, master, rank, slot_order, gains)
+        in_specs = [hbm, hbm, vm, sm, sm, vm]
+        middle = sds((n // 8, BLK, BLK), f32)
         extra = [
             pltpu.VMEM((parts, D, 3 * hm), bf16),
+            pltpu.VMEM((parts, hm, D), bf16),
             pltpu.VMEM((parts, D, fm), bf16),
-            pltpu.VMEM((parts, hm, D), bf16),
             pltpu.VMEM((parts, fm, D), bf16),
-            pltpu.VMEM((rank.shape[0], BLK, BLK), bf16),
-            pltpu.SemaphoreType.DMA((128,)),
-            pltpu.SemaphoreType.DMA((128,)),
+            pltpu.VMEM((parts, D, wide), bf16),
+            pltpu.VMEM((n, BLK, BLK), bf16),
+            pltpu.VMEM((n, BLK, BLK), bf16),
+            pltpu.VMEM((n // 2, BLK, BLK), bf16),
+            pltpu.VMEM((3, n // 8, BLK, BLK), bf16),
+            pltpu.VMEM((3, D // 2, wide), bf16),
+            pltpu.VMEM((3, 3, D // 8, wide), bf16),
+            pltpu.VMEM((3, D // 8, wide), bf16),
+            pltpu.VMEM((parts, 8, D), f32),
+            pltpu.VMEM((4, 8, D), f32),
+            pltpu.VMEM((2, 8, D), f32),
+            pltpu.SemaphoreType.DMA((256,)),
+            pltpu.SemaphoreType.DMA((256,)),
         ]
         params = dict(collective_id=0, has_side_effects=True)
     else:
-        args = (tokens, cotangent, *weights, gains)
-        in_specs = [vm] * 7
+        args = (tokens, cotangent, base, *weights, gains)
+        in_specs = [hbm, hbm, sm] + [vm] * 5
+        middle = sds((parts, D, wide), bf16)
         extra = []
         params = {}
     return pl.pallas_call(
         functools.partial(compute_kernel, linked),
-        out_shape=(
-            sds((L, D), bf16),
-            sds((L, D), f32),
-            sds((parts, D, 3 * hm), grad_type),
-            sds((parts, D, fm), grad_type),
-            sds((parts, D, hm), grad_type),
-            sds((parts, D, fm), grad_type),
-            sds((8, D), f32),
-        ),
+        out_shape=(sds((L, D), bf16), sds((L, D), f32), middle, sds((8, D), f32)),
         in_specs=in_specs,
-        out_specs=[vm] * 7,
-        scratch_shapes=extra + [
-            pltpu.VMEM((L, D), bf16),
-            pltpu.VMEM((D, L), bf16),
-            pltpu.VMEM((L, D), bf16),
-            pltpu.VMEM((D, L), bf16),
-            pltpu.VMEM((L, D), bf16),
-            pltpu.VMEM((D, L), bf16),
-            pltpu.VMEM((L, D), bf16),
-            pltpu.VMEM((D, L), bf16),
-            pltpu.VMEM((parts, L, hm), f32),
-            pltpu.VMEM((parts, L, hm), f32),
-            pltpu.VMEM((parts, L, hm), f32),
-            pltpu.VMEM((parts, L, hm), f32),
-            pltpu.VMEM((2 * hm // BLK, L, BLK), f32),
-            pltpu.VMEM((L, D), f32),
-            pltpu.VMEM((L, D), f32),
-            pltpu.VMEM((L, D), f32),
-            pltpu.VMEM((L, fm), bf16),
-            pltpu.VMEM((L, fm), bf16),
-            pltpu.VMEM((L, 3 * hm), bf16),
+        out_specs=[hbm, hbm, vm, vm],
+        scratch_shapes=extra
+        + [pltpu.VMEM(shape, bf16) for shape in ((L, D), (D, L)) * 3]
+        + [pltpu.VMEM((parts, L, hm), f32)] * 4
+        + [pltpu.VMEM((2 * hm // BLK, L, BLK), f32)]
+        + [pltpu.VMEM((L, D), f32)] * 3
+        + [
+            pltpu.VMEM((L, 2 * fm), bf16),
             pltpu.VMEM((2, SUB, hm), f32),
+            pltpu.SemaphoreType.DMA((3,)),
         ],
-        compiler_params=pltpu.CompilerParams(vmem_limit_bytes=63 * 2**20, **params),
+        compiler_params=pltpu.CompilerParams(vmem_limit_bytes=64 * 2**20 - 2**16, **params),
         name="block",
     )(*args)
 
@@ -569,14 +766,66 @@
     return (first_new, second_new, first_hat / (jnp.sqrt(second_hat) + adam_eps))
 
 
-def soap_update(master, moment_one, moment_two, basis_left, basis_right, grads):
-    left_side = jnp.einsum("pkab,pkac->pkbc", basis_left, grads, precision=highest)
-    rotated = jnp.einsum("pkbc,pkcd->pkbd", left_side, basis_right, precision=highest)
-    first_new, second_new, direction = adam_update(moment_one, moment_two, rotated)
-    turned = jnp.einsum("pkab,pkbc->pkac", basis_left, direction, precision=highest)
-    turned = jnp.einsum("pkac,pkdc->pkad", turned, basis_right, precision=highest)
-    master_new = master - learn_rate * (turned + weight_decay * master)
-    return (first_new, second_new, master_new)
+def fine_dot(a, b, trans_b=False):
+    a_high, b_high = a.astype(bf16), b.astype(bf16)
+    a_low, b_low = (a - a_high.astype(f32)).astype(bf16), (b - b_high.astype(f32)).astype(bf16)
+    return dot(a_high, b_high, trans_b) + (dot(a_high, b_low, trans_b) + dot(a_low, b_high, trans_b))
+
+
+def update_kernel(
+    low_first,
+    token_total,
+    low,
+    owned,
+    master,
+    moment_one,
+    moment_two,
+    basis_left,
+    basis_right,
+    sums,
+    gains,
+    gain_moment_one,
+    gain_moment_two,
+    first_new,
+    second_new,
+    master_new,
+    master_low,
+    gain_first,
+    gain_second,
+    gains_new,
+    forget_mean,
+):
+    for s in range(master.shape[0]):
+        grad = owned[s]
+        grad = jnp.where(low[s] >= low_first, grad.T, grad)
+        left, right = basis_left[s], basis_right[s]
+        rotated = fine_dot(fine_dot(left.T, grad), right)
+        first, second, direction = adam_update(moment_one[s], moment_two[s], rotated)
+        first_new[s] = first
+        second_new[s] = second
+        turned = fine_dot(fine_dot(left, direction), right, True)
+        fresh = master[s] - learn_rate * (turned + weight_decay * master[s])
+        master_new[s] = fresh
+        master_low[s] = fresh.astype(bf16)
+    first, second, direction = adam_update(gain_moment_one[...], gain_moment_two[...], sums[0:2, :])
+    gain_first[...] = first
+    gain_second[...] = second
+    gains_new[...] = gains[...] - gain_rate * direction
+    forget_mean[...] = jnp.sum(sums[2:3, :], axis=1, keepdims=True) * (1.0 / (H * (token_total + 1) / 2.0))
+
+
+def update(low_first, token_total, *args):
+    sds = jax.ShapeDtypeStruct
+    blocks, gain = args[1].shape, args[8].shape
+    vm = pl.BlockSpec(memory_space=pltpu.VMEM)
+    return pl.pallas_call(
+        functools.partial(update_kernel, low_first, token_total),
+        out_shape=[sds(blocks, f32)] * 3 + [sds(blocks, bf16)] + [sds(gain, f32)] * 3 + [sds((1, 1), f32)],
+        in_specs=[pl.BlockSpec(memory_space=pltpu.SMEM)] + [vm] * (len(args) - 1),
+        out_specs=[vm] * 8,
+        compiler_params=pltpu.CompilerParams(vmem_limit_bytes=32 * 2**20),
+        name="update",
+    )(*args)
 
 
 def on_device(
@@ -597,12 +846,15 @@
     hm, fm = H // parts, FF // parts
     token_total = L * data_parts * parts
     row_tiles, cols, lows = D // BLK, (3 * hm + fm) // BLK, (hm + fm) // BLK
-    number = jnp.arange(owner.shape[0], dtype=jnp.int32)
+    blocks = owner.shape[0]
+    number = jnp.arange(blocks, dtype=jnp.int32)
     ahead = (owner[None, :] < owner[:, None]) | ((owner[None, :] == owner[:, None]) & (number[None, :] < number[:, None]))
     block_rank = jnp.sum(ahead.astype(jnp.int32), axis=1)
     slot_order = jnp.sum(jnp.where(block_rank[None, :] == number[:, None], number[None, :], 0), axis=1)
     if data_parts == 8 and parts == 4:
-        outs = compute(tokens, cotangent, gains, bf16, master=master[0], rank=block_rank)
+        block_out, input_grad, owned, sums = compute(
+            tokens, cotangent, gains, master=master[0], rank=block_rank, slot_order=slot_order
+        )
     else:
         stored = lax.all_gather(master.astype(bf16), "dp", axis=1, tiled=True)
         stored = lax.all_gather(stored, "mp", axis=0, tiled=True)
@@ -611,34 +863,47 @@
         upper = upper.transpose(0, 1, 3, 2, 4).reshape(parts, D, cols * BLK)
         lower = stack[:, row_tiles * cols :].reshape(parts, lows, row_tiles, BLK, BLK)
         lower = lower.transpose(0, 1, 3, 2, 4).reshape(parts, lows * BLK, D)
-        weights = (upper[:, :, : 3 * hm], upper[:, :, 3 * hm :], lower[:, :hm], lower[:, hm:])
-        outs = compute(tokens, cotangent, gains, bf16, weights=weights)
-    block_out, input_grad, gg, gu, go, gd, small = outs
-    upper = jnp.concatenate([gg, gu], axis=2).reshape(parts, row_tiles, BLK, cols, BLK).transpose(0, 1, 3, 2, 4)
-    upper = upper.reshape(parts, row_tiles * cols, BLK, BLK)
-    lower = jnp.concatenate([go, gd], axis=2).reshape(parts, row_tiles, BLK, lows, BLK).transpose(0, 3, 1, 4, 2)
-    lower = lower.reshape(parts, row_tiles * lows, BLK, BLK)
-    natural = jnp.concatenate([upper, lower], axis=1).astype(f32)
-    owned = lax.psum_scatter(natural[:, slot_order], "dp", scatter_dimension=1, tiled=True)
-    owned = lax.psum_scatter(owned, "mp", scatter_dimension=0, tiled=True)
-    first_new, second_new, master_new = soap_update(master, moment_one, moment_two, basis_left, basis_right, owned)
-    first_row = (lax.axis_index("dp") * parts + lax.axis_index("mp")) * L
-    forget_part = (jnp.sum(small[3, :hm]) + (first_row + 1).astype(f32) * jnp.sum(small[2, :hm])) / float(token_total)
-    gain_grad, forget_total = lax.psum((small[:2], forget_part), ("dp", "mp"))
-    gain_first, gain_second, gain_direction = adam_update(gain_moment_one, gain_moment_two, gain_grad)
-    gains_new = gains - gain_rate * gain_direction
-    forget_mean = forget_total / (H * (token_total + 1) / 2.0)
+        weights = (upper[:, :, : 3 * hm], lower[:, :hm], upper[:, :, 3 * hm :], lower[:, hm:])
+        first = ((lax.axis_index("dp") * parts + lax.axis_index("mp")) * L + 1).astype(f32)
+        base = jnp.stack([first, jnp.asarray(token_total, f32)])
+        block_out, input_grad, grads, sums = compute(tokens, cotangent, gains, weights=weights, base=base)
+        upper = jnp.concatenate([grads[:, :, : 3 * hm], grads[:, :, 4 * hm : 4 * hm + fm]], axis=2)
+        upper = upper.reshape(parts, row_tiles, BLK, cols, BLK).transpose(0, 1, 3, 2, 4)
+        lower = jnp.concatenate([grads[:, :, 3 * hm : 4 * hm], grads[:, :, 4 * hm + fm :]], axis=2)
+        lower = lower.reshape(parts, row_tiles, BLK, lows, BLK).transpose(0, 3, 1, 2, 4)
+        natural = jnp.concatenate(
+            [upper.reshape(parts, -1, BLK, BLK), lower.reshape(parts, -1, BLK, BLK)], axis=1
+        ).astype(f32)
+        owned = lax.psum_scatter(natural[:, slot_order], "dp", scatter_dimension=1, tiled=True)
+        owned = lax.psum_scatter(owned, "mp", scatter_dimension=0, tiled=True)[0]
+        sums = lax.psum(sums, ("dp", "mp"))
+    mine = lax.dynamic_slice_in_dim(slot_order, lax.axis_index("dp") * master.shape[1], master.shape[1])
+    first_new, second_new, master_new, master_low, gain_first, gain_second, gains_new, forget_mean = update(
+        row_tiles * cols,
+        token_total,
+        mine,
+        owned,
+        master[0],
+        moment_one[0],
+        moment_two[0],
+        basis_left[0],
+        basis_right[0],
+        sums,
+        gains,
+        gain_moment_one,
+        gain_moment_two,
+    )
     return (
         block_out,
         input_grad,
-        first_new,
-        second_new,
-        master_new,
-        master_new.astype(bf16),
+        first_new[None],
+        second_new[None],
+        master_new[None],
+        master_low[None],
         gain_first,
         gain_second,
         gains_new,
-        forget_mean,
+        forget_mean[0, 0],
     )
 
 

time: 417 us -> 159 us (0.38)
  waiting for transfers between devices: 157 us -> 0 us
  local copies, waits for them, and re-layouts: 58.8 us -> 12.6 us
  blocking collectives: 43.3 us -> 0 us
  Pallas kernels: 112 us -> 144 us
  other arithmetic: 19.7 us -> 1.53 us
  between operations: 17.3 us -> 0.68 us
  matrix products: 7.63 us -> 0 us
    reduce_scatter x1 -> x0, waiting for transfers between devices: 115 us -> none  [on_device(): lax.psum_scatter(natural[:, slot_order], 'dp', scatter_dimension=1, tiled...]
    psum x1 -> x0, blocking collectives: 43.3 us -> none  [on_device(): gain_grad, forget_total = lax.psum((small[:2], forget_part), ('dp', 'mp'))]
    unnamed x3 -> x0, waiting for transfers between devices: 41.2 us -> none
    pallas_call x1, Pallas kernels: 112 us -> 139 us  [compute(): pl.pallas_call(functools.partial(compute_kernel, linked), out_shape=(sds(...]
    gather x1 -> x0, local copies, waits for them, and re-layouts: 14.6 us -> none  [on_device(): natural[:, slot_order]]
    reshape x2 -> x0, local copies, waits for them, and re-layouts: 14 us -> none  [the longest x1 8.31 us: on_device(): jnp.concatenate([gg, gu], axis=2).reshape(parts, row_tiles, BLK, cols, BLK)]
    transpose x2 -> x0, local copies, waits for them, and re-layouts: 13.5 us -> none  [the longest x1 8.9 us: on_device(): jnp.concatenate([gg, gu], axis=2).reshape(parts, row_tiles, BLK, cols, BLK)]
    concatenate x2 -> x0, local copies, waits for them, and re-layouts: 12.6 us -> none  [the longest x1 7.86 us: on_device(): jnp.concatenate([gg, gu], axis=2).reshape(parts, row_tiles, BLK, cols, BLK)]
  transfers between devices with their start and end apart: 2 -> 0, of which waited for: 2 -> 0; matrix products, arithmetic and copies ran while one was open for 1% -> 0% of each run, Pallas kernels for 0% -> 0%
where the time goes in v3:
time: 159 us
  Pallas kernels  144 us (91%)
  local copies, waits for them, and re-layouts  12.6 us (8%)
    pallas_call x1, Pallas kernels, compute(): pl.pallas_call(functools.partial(compute_kernel, linked), out_shape=(sds(...  139 us
    unnamed x28, local copies, waits for them, and re-layouts  11.8 us
    pallas_call x1, Pallas kernels, update(): pl.pallas_call(functools.partial(update_kernel, low_first, token_total),...  5.54 us

profile of v3, /device:TPU:0, one launch (start us, length us, event | category | flops | bytes accessed | tf_op | source)
XLA Modules:
  0.0 158.9 jit_solution(9176281929049134513)
XLA Ops:
  0.6 0.9 convert_reduce_fusion.refs_3_
  1.6 0.0 copy-start.12
  1.6 0.5 copy-done.12
  2.1 0.6 select_reduce_fusion.refs_4_
  2.7 138.5 %block.1 = (bf16[1024,512]{1,0:T(8,128)(2,1)}, f32[1024,512]{1,0:T(8,128)}, f32[8,128,128]{2,1,0:T(8,128)}, f32[8,512]{1,0:T(8,128)}) custom-call(bf16[1024,512]{1,0:T(8,128)(2,1)} %refs_0_.1, bf16[1024,512]{1,0:T(8,128)(2,1)} %refs_1_.1, f32[8,128,128]{2,1,0:T(8,128)} %bitcast.10, s32[64]{0:T(128)} %copy-done.12, s32[64]{0:T(128)} %select_reduce_fusion.refs_4_, ...), custom_call_target="tpu_custom_call" | custom-call | tf_op jit(solution)/shard_map/block/pallas_call | solution.py:741
  141.3 0.7 dynamic_slice.3.low
  142.0 0.0 copy-start
  142.0 1.0 copy-done
  143.0 0.0 copy-start.1
  143.0 1.0 copy-done.1
  144.1 0.0 copy-start.2
  144.1 1.0 copy-done.2
  145.1 0.0 copy-start.3
  145.1 1.0 copy-done.3
  146.2 0.0 copy-start.4
  146.2 1.0 copy-done.4
  147.2 0.0 copy-start.5
  147.2 1.0 copy-done.5
  148.2 0.0 copy-start.6
  148.2 0.7 copy-done.6
  149.0 0.0 copy-start.7
  149.0 0.7 copy-done.7
  149.6 0.0 copy-start.8
  149.6 0.7 copy-done.8
  150.3 0.0 copy-start.9
  150.3 0.7 copy-done.9
  151.0 0.0 copy-start.11
  151.0 0.0 copy-start.10
  151.0 5.5 %update.1 = (f32[8,128,128]{2,1,0:T(8,128)}, f32[8,128,128]{2,1,0:T(8,128)}, f32[8,128,128]{2,1,0:T(8,128)}, bf16[8,128,128]{2,1,0:T(8,128)(2,1)}, f32[2,512]{1,...) custom-call(s32[8]{0:T(128)S(1)} %dynamic_slice.3.low, f32[8,128,128]{2,1,0:T(8,128)S(1)} %copy-done.5, ...), custom_call_target="tpu_custom_call" | custom-call | tf_op jit(solution)/shard_map/update/pallas_call | solution.py:821
  156.6 0.0 copy-done.11
  156.6 1.0 copy.23
  157.5 0.0 copy-done.10
  157.5 1.3 copy.24
Async XLA Ops:
  1.6 0.5 copy-start.12
  142.0 1.0 copy-start
  143.0 1.0 copy-start.1
  144.1 1.0 copy-start.2
  145.1 1.0 copy-start.3
  146.2 1.0 copy-start.4
  147.2 1.0 copy-start.5
  148.2 0.7 copy-start.6
  149.0 0.7 copy-start.7
  149.6 0.7 copy-start.8
  150.3 0.7 copy-start.9
  151.0 5.6 %copy-start.11 = (bf16[1024,512]{1,0:T(8,128)(2,1)S(1)}, bf16[1024,512]{1,0:T(8,128)(2,1)}, u32[]{:S(2)}) copy-start(bf16[1024,512]{1,0:T(8,128)(2,1)} %get-tuple-element.44) | copy-start | bytes 3145732
  151.0 6.5 %copy-start.10 = (f32[1024,512]{1,0:T(8,128)S(1)}, f32[1024,512]{1,0:T(8,128)}, u32[]{:S(2)}) copy-start(f32[1024,512]{1,0:T(8,128)} %get-tuple-element.45) | copy-start | bytes 6291460

commit v4 on v3

--- a/solution.py
+++ b/solution.py
@@ -109,6 +109,7 @@
         self.core = d + 1 - 2 * core
         self.plane = [d + 2 - 4 * col, d + 4 - 8 * row, d + 6 - 4 * col - 8 * row]
         self.order = [m, m + 1 - 2 * (m % 2), m + 2 - 4 * (m // 2), 3 - m]
+        self.along, self.spreads = {}, {}
         barrier = pltpu.get_barrier_semaphore()
         for device in [(e, m) for e in [self.core] + self.plane] + [(d, k) for k in self.order[1:]]:
             pl.semaphore_signal(barrier, inc=1, device_id=device, device_id_type=MESH)
@@ -175,14 +176,11 @@
         size = ref.shape[1] // 8
         return ref.at[k, pl.ds(pl.multiple_of(e * size, size), size)]
 
-    def along_start(self, kind):
-        self.along = getattr(self, "along", {})
-        for i in (1, 2, 3):
-            ref = self.share(kind, self.m, self.me)
-            self.along[kind, i] = self.net.start(ref, ref, (self.me, self.order[i]))
+    def along_start(self, kind, i):
+        ref = self.share(kind, self.m, self.me)
+        self.along[kind, i] = self.net.start(ref, ref, (self.me, self.order[i]))
 
     def spread(self, kind, i):
-        self.spreads = getattr(self, "spreads", {})
         self.along[kind, i].wait_recv()
         ref = self.share(kind, self.order[i], self.me)
         self.spreads[kind, i] = (
@@ -280,23 +278,51 @@
 
     def slots_plane(self, out, pair, far):
         g, n = self.g, out.shape[0] // 8
-        self.ends = []
-        for copy, e, k in zip(self.last, (g.plane[2], g.plane[0], g.plane[1]), (2, 0, 1)):
-            copy.wait_recv()
-            rows = pl.ds((g.side * 4 + e // 2) * n, n)
+        h = n // 2
+        x, y, z = g.plane
+        wait = dict(zip("zxyo", self.last))
+
+        def mine(e, first, count):
+            return pl.ds((g.side * 4 + e // 2) * n + first, count)
+
+        def join(e):
+            rows = mine(e, 0, n)
             out[rows] = (out[rows].astype(f32) + pair[pl.ds((e // 2) * n, n)].astype(f32)).astype(bf16)
-            self.ends.append(self.net.start(out.at[rows], far.at[k], (e, g.m)))
-        self.last[3].wait_recv()
+
+        def send(e, first, slot, to):
+            return self.net.start(out.at[mine(e, first, h)], far.at[slot], (to, g.m))
+
+        wait["z"].wait_recv()
+        join(z)
+        over_x = send(z, 0, 0, x)
+        over_y = send(z, h, 1, y)
+        wait["x"].wait_recv()
+        join(x)
+        self.ends = [send(x, 0, 2, x)]
+        wait["y"].wait_recv()
+        join(y)
+        self.ends.append(send(y, h, 3, y))
+        over_x.wait_recv()
+        rows = mine(y, 0, h)
+        out[rows] = (out[rows].astype(f32) + far[0].astype(f32)).astype(bf16)
+        self.ends.append(send(y, 0, 4, y))
+        over_y.wait_recv()
+        rows = mine(x, h, h)
+        out[rows] = (out[rows].astype(f32) + far[1].astype(f32)).astype(bf16)
+        self.ends.append(send(x, h, 5, x))
+        wait["o"].wait_recv()
 
     def slots_end(self, out, pair, far, owned):
         g, n = self.g, out.shape[0] // 8
-        total = out[pl.ds((g.side * 4 + g.me // 2) * n, n)].astype(f32)
-        total += pair[pl.ds((g.me // 2) * n, n)].astype(f32)
+        h = n // 2
         for copy in self.ends:
             copy.wait_recv()
-        for k in range(3):
-            total += far[k].astype(f32)
-        owned[...] = total
+        for first, slots in ((0, (2, 4)), (h, (3, 5))):
+            total = out[pl.ds((g.side * 4 + g.me // 2) * n + first, h)].astype(f32)
+            total += pair[pl.ds((g.me // 2) * n + first, h)].astype(f32)
+            for k in slots:
+                total += far[k].astype(f32)
+            owned[first : first + h] = total
 
 
 class SmallSum:
@@ -350,8 +376,8 @@
 
     fetch_cot = pltpu.make_async_copy(cotangent, cot, local.at[0])
     fetch_tok = pltpu.make_async_copy(tokens, n1, local.at[1])
+    fetch_tok.start()
     fetch_cot.start()
-    fetch_tok.start()
 
     def permute_in(src, dst):
         for k in range(D // BLK):
@@ -392,9 +418,6 @@
     else:
         order = list(range(parts))
 
-    fetch_cot.wait()
-    permute_in(cot, cot)
-    cott[...] = cot[...].T
     fetch_tok.wait()
     permute_in(n1, n1)
     mixed[...] = n1[...].astype(f32)
@@ -411,10 +434,9 @@
     if linked:
         gather.plane_finish()
         gather.place((0,))
-        gather.along_start(0)
+        for i in (1, 2, 3):
+            gather.along_start(0, i)
         gather.place((1, 2, 3))
-        for kind in (1, 2, 3):
-            gather.along_start(kind)
 
     fills[0] = jnp.zeros((SUB, hm), f32)
     fills[1] = jnp.ones((SUB, hm), f32)
@@ -434,17 +456,10 @@
             cand[m, rows, :] = dot(x, wg[m, :, 2 * hm :])
 
         if linked and turn == 0:
-            for i in (1, 2, 3):
-                gather.spread(0, i)
+            gather.spread(0, 1)
+        if linked and turn == 1:
+            gather.pair(0, 2)
         if linked and turn == 2:
-            gather.pair(0, 3)
-        if linked and turn == 1:
-            for i in (1, 2, 3):
-                gather.spread(1, i)
-        if linked and turn == 2:
-            for kind, i in ((2, 1), (3, 1), (2, 2), (3, 2), (2, 3), (3, 3)):
-                gather.spread(kind, i)
-        if linked and turn == 3:
             for i in (1, 2, 3):
                 gather.pair(1, i)
 
@@ -474,21 +489,45 @@
         for _ in range(SUB - 1):
             enter = shift_down(s + p * enter)
 
-        if linked and turn == 0:
-            gather.pair(0, 1)
-        if linked and turn == 1:
-            gather.pair(0, 2)
+        if linked:
+            if turn == 0:
+                gather.spread(0, 2)
+            if turn == 1:
+                gather.pair(0, 3)
+                for i in (1, 2, 3):
+                    gather.spread(1, i)
+            if turn == 2:
+                gather.spread(2, 1)
+                gather.spread(3, 1)
+            if turn == 3:
+                gather.pair(2, 1)
+                gather.pair(3, 1)
+                gather.spread(2, 2)
+                gather.spread(3, 2)
+            if turn:
+                gather.along_start(2, turn)
+                gather.along_start(3, turn)
 
         @pl.loop(0, J, unroll=4)
         def _(j):
             rows = pl.ds(pl.multiple_of(j * SUB, SUB), SUB)
             state[m, rows, :] = take(0, rows) + take(half, rows) * enter
 
+        if turn == 0:
+            fetch_cot.wait()
+            permute_in(cot, cot)
+            if linked:
+                gather.pair(0, 1)
+                gather.spread(0, 3)
+                for i in (1, 2, 3):
+                    gather.along_start(1, i)
+            cott[...] = cot[...].T
+
     if linked:
         for i in (1, 2, 3):
             gather.ready(1, i)
         for kind in (2, 3):
-            gather.pair(kind, 1)
+            gather.spread(kind, 3)
 
     @pl.loop(0, L // R)
     def _(i):
@@ -532,6 +571,7 @@
         if linked and turn == 3:
             reduce.model(2, 1)
             reduce.model(3, 1)
+            net.drain()
         grads[m, :, downs] = dot(cott[...], act[...]).astype(bf16)
         grads[m, :, ups] = dot(n2t[...], dup[...]).astype(bf16)
         if linked and turn:
@@ -567,6 +607,11 @@
     fetch_tok.start()
 
     for turn, m in reversed(list(enumerate(order))):
+        grads[m, :, outs] = dot(dmlt[...], state[m].astype(bf16)).astype(bf16)
+        if linked and turn:
+            reduce.chip(1, turn)
+
+    for turn, m in reversed(list(enumerate(order))):
 
         @pl.loop(0, L // R)
         def _(i):
@@ -594,6 +639,23 @@
         enter = fills[0]
         for _ in range(SUB - 1):
             enter = shift_up(keep_first * (u + p * enter))
+
+        if linked:
+            if turn == 3:
+                for kind in (2, 3):
+                    reduce.model(kind, 3)
+                for i in (3, 2, 1):
+                    reduce.plane(1, i)
+            if turn < 3:
+                reduce.plane(0, turn + 1)
+            if turn == 2:
+                for i in (3, 2, 1):
+                    reduce.model(1, i)
+            if turn < 2:
+                reduce.model(0, turn + 2)
+            if turn == 0:
+                for kind in (1, 2, 3):
+                    reduce.own(kind)
 
         def back(i, before):
             parts_out = []
@@ -617,24 +679,9 @@
         last = state[m, pl.ds(L - SUB, SUB), :]
         lax.fori_loop(0, J // 2, back, shift_down(last), unroll=2)
 
-        if linked:
-            if turn == 3:
-                for kind in (2, 3):
-                    reduce.model(kind, 3)
-            if turn == 1:
-                for kind in (0, 1):
-                    reduce.model(kind, 3)
-            if turn == 0:
-                for kind in (0, 1):
-                    reduce.model(kind, 2)
-            if turn < 3:
-                for kind in (0, 1):
-                    reduce.plane(kind, turn + 1)
         grads[m, :, gate] = dot(n1t[...], dpre[...]).astype(bf16)
-        grads[m, :, outs] = dot(dmlt[...], state[m].astype(bf16)).astype(bf16)
         if linked and turn:
-            for kind in (0, 1):
-                reduce.chip(kind, turn)
+            reduce.chip(0, turn)
 
         @pl.loop(0, L // R)
         def _(i):
@@ -645,10 +692,7 @@
     permute_in(cot, cot)
 
     if linked:
-        for kind in (0, 1):
-            reduce.model(kind, 1)
-        for kind in (2, 3):
-            reduce.own(kind)
+        reduce.model(0, 1)
 
     def back_one(i, total):
         rows = pl.ds(pl.multiple_of(i * R, R), R)
@@ -677,9 +721,7 @@
     if linked:
         tiny = SmallSum(net, gather, small, sum_a, sum_b, sum_c)
         tiny.send(0)
-        for kind in (0, 1):
-            reduce.own(kind)
-        net.drain()
+        reduce.own(0)
         reduce.into_slots(slots, turned, slot_order)
         reduce.slots_chip(turned, pair)
         tiny.add(0)
@@ -721,7 +763,7 @@
             pltpu.VMEM((n, BLK, BLK), bf16),
             pltpu.VMEM((n, BLK, BLK), bf16),
             pltpu.VMEM((n // 2, BLK, BLK), bf16),
-            pltpu.VMEM((3, n // 8, BLK, BLK), bf16),
+            pltpu.VMEM((6, n // 16, BLK, BLK), bf16),
             pltpu.VMEM((3, D // 2, wide), bf16),
             pltpu.VMEM((3, 3, D // 8, wide), bf16),
             pltpu.VMEM((3, D // 8, wide), bf16),
@@ -775,57 +817,92 @@
 def update_kernel(
     low_first,
     token_total,
+    passed,
     low,
+    sums,
+    gains,
+    gain_moment_one,
+    gain_moment_two,
     owned,
     master,
     moment_one,
     moment_two,
     basis_left,
     basis_right,
-    sums,
-    gains,
-    gain_moment_one,
-    gain_moment_two,
-    first_new,
-    second_new,
-    master_new,
-    master_low,
-    gain_first,
-    gain_second,
-    gains_new,
-    forget_mean,
+    *refs,
 ):
-    for s in range(master.shape[0]):
-        grad = owned[s]
+    given, refs = refs[:passed], refs[passed:]
+    first_new, second_new, master_new, master_low, gain_first, gain_second, gains_new, forget_mean = refs[:8]
+    copied, refs = refs[8 : 8 + passed], refs[8 + passed :]
+    held, made, made_low, sem_in, sem_out, sem_pass = refs
+    count = master.shape[0]
+    passing = [pltpu.make_async_copy(src, dst, sem_pass.at[k]) for k, (src, dst) in enumerate(zip(given, copied))]
+    sources = (owned, basis_left, basis_right, moment_one, moment_two, master)
+    fetch = [
+        [pltpu.make_async_copy(src.at[s], held.at[s, k], sem_in.at[s, k]) for k, src in enumerate(sources)]
+        for s in range(count)
+    ]
+    for row in fetch:
+        for copy in row:
+            copy.start()
+    for copy in passing:
+        copy.start()
+    push = []
+    for s in range(count):
+        for copy in fetch[s]:
+            copy.wait()
+        grad = held[s, 0]
         grad = jnp.where(low[s] >= low_first, grad.T, grad)
-        left, right = basis_left[s], basis_right[s]
+        left, right = held[s, 1], held[s, 2]
         rotated = fine_dot(fine_dot(left.T, grad), right)
-        first, second, direction = adam_update(moment_one[s], moment_two[s], rotated)
-        first_new[s] = first
-        second_new[s] = second
+        first, second, direction = adam_update(held[s, 3], held[s, 4], rotated)
+        made[s, 0] = first
+        made[s, 1] = second
         turned = fine_dot(fine_dot(left, direction), right, True)
-        fresh = master[s] - learn_rate * (turned + weight_decay * master[s])
-        master_new[s] = fresh
-        master_low[s] = fresh.astype(bf16)
+        old = held[s, 5]
+        fresh = old - learn_rate * (turned + weight_decay * old)
+        made[s, 2] = fresh
+        made_low[s] = fresh.astype(bf16)
+        for k, (src, dst) in enumerate(
+            ((made.at[s, 0], first_new), (made.at[s, 1], second_new), (made.at[s, 2], master_new), (made_low.at[s], master_low))
+        ):
+            copy = pltpu.make_async_copy(src, dst.at[s], sem_out.at[s, k])
+            copy.start()
+            push.append(copy)
     first, second, direction = adam_update(gain_moment_one[...], gain_moment_two[...], sums[0:2, :])
     gain_first[...] = first
     gain_second[...] = second
     gains_new[...] = gains[...] - gain_rate * direction
     forget_mean[...] = jnp.sum(sums[2:3, :], axis=1, keepdims=True) * (1.0 / (H * (token_total + 1) / 2.0))
-
-
-def update(low_first, token_total, *args):
+    for copy in push + passing:
+        copy.wait()
+
+
+def update(low_first, token_total, small, large, passed):
     sds = jax.ShapeDtypeStruct
-    blocks, gain = args[1].shape, args[8].shape
-    vm = pl.BlockSpec(memory_space=pltpu.VMEM)
+    blocks, gain = large[0].shape, small[2].shape
+    vm, hbm = pl.BlockSpec(memory_space=pltpu.VMEM), pl.BlockSpec(memory_space=pl.ANY)
+    count = blocks[0]
     return pl.pallas_call(
-        functools.partial(update_kernel, low_first, token_total),
-        out_shape=[sds(blocks, f32)] * 3 + [sds(blocks, bf16)] + [sds(gain, f32)] * 3 + [sds((1, 1), f32)],
-        in_specs=[pl.BlockSpec(memory_space=pltpu.SMEM)] + [vm] * (len(args) - 1),
-        out_specs=[vm] * 8,
-        compiler_params=pltpu.CompilerParams(vmem_limit_bytes=32 * 2**20),
+        functools.partial(update_kernel, low_first, token_total, len(passed)),
+        out_shape=[sds(blocks, f32)] * 3
+        + [sds(blocks, bf16)]
+        + [sds(gain, f32)] * 3
+        + [sds((1, 1), f32)]
+        + [sds(v.shape, v.dtype) for v in passed],
+        in_specs=[pl.BlockSpec(memory_space=pltpu.SMEM)] + [vm] * 4 + [hbm] * (len(large) + len(passed)),
+        out_specs=[hbm] * 4 + [vm] * 4 + [hbm] * len(passed),
+        scratch_shapes=[
+            pltpu.VMEM((count, 6, BLK, BLK), f32),
+            pltpu.VMEM((count, 3, BLK, BLK), f32),
+            pltpu.VMEM((count, BLK, BLK), bf16),
+            pltpu.SemaphoreType.DMA((count, 6)),
+            pltpu.SemaphoreType.DMA((count, 4)),
+            pltpu.SemaphoreType.DMA((max(len(passed), 1),)),
+        ],
+        compiler_params=pltpu.CompilerParams(vmem_limit_bytes=56 * 2**20),
         name="update",
-    )(*args)
+    )(*small, *large, *passed)
 
 
 def on_device(
@@ -878,21 +955,15 @@
         owned = lax.psum_scatter(owned, "mp", scatter_dimension=0, tiled=True)[0]
         sums = lax.psum(sums, ("dp", "mp"))
     mine = lax.dynamic_slice_in_dim(slot_order, lax.axis_index("dp") * master.shape[1], master.shape[1])
-    first_new, second_new, master_new, master_low, gain_first, gain_second, gains_new, forget_mean = update(
+    outs = update(
         row_tiles * cols,
         token_total,
-        mine,
-        owned,
-        master[0],
-        moment_one[0],
-        moment_two[0],
-        basis_left[0],
-        basis_right[0],
-        sums,
-        gains,
-        gain_moment_one,
-        gain_moment_two,
+        (mine, sums, gains, gain_moment_one, gain_moment_two),
+        (owned, master[0], moment_one[0], moment_two[0], basis_left[0], basis_right[0]),
+        (block_out, input_grad),
     )
+    first_new, second_new, master_new, master_low, gain_first, gain_second, gains_new, forget_mean = outs[:8]
+    block_out, input_grad = outs[8:]
     return (
         block_out,
         input_grad,

time: 159 us -> 247 us (1.55)
  Pallas kernels: 144 us -> 244 us
  local copies, waits for them, and re-layouts: 12.6 us -> 1.69 us
    pallas_call x1, Pallas kernels: 5.54 us -> 98.6 us  [update(): pl.pallas_call(functools.partial(update_kernel, low_first, token_total, l...]
    unnamed x28 -> x4, local copies, waits for them, and re-layouts: 11.8 us -> 1.02 us
    pallas_call x1, Pallas kernels: 139 us -> 145 us  [compute(): pl.pallas_call(functools.partial(compute_kernel, linked), out_shape=(sds(...]
where the time goes in v4:
time: 247 us
  Pallas kernels  244 us (99%)
    pallas_call x1, Pallas kernels, compute(): pl.pallas_call(functools.partial(compute_kernel, linked), out_shape=(sds(...  145 us
    pallas_call x1, Pallas kernels, update(): pl.pallas_call(functools.partial(update_kernel, low_first, token_total, l...  98.6 us

profile of v4, /device:TPU:0, one launch (start us, length us, event | category | flops | bytes accessed | tf_op | source)
XLA Modules:
  0.0 247.1 jit_solution(553576637159822969)
XLA Ops:
  0.6 0.9 convert_reduce_fusion.refs_3_
  1.6 0.0 copy-start
  1.6 0.5 copy-done
  2.1 0.1 select_reduce_fusion.refs_4_
  2.2 0.0 copy-start.1
  2.2 0.5 copy-done.1
  2.7 0.7 dynamic_slice.3.low
  3.4 144.9 %block.1 = (bf16[1024,512]{1,0:T(8,128)(2,1)}, f32[1024,512]{1,0:T(8,128)}, f32[8,128,128]{2,1,0:T(8,128)}, f32[8,512]{1,0:T(8,128)}) custom-call(bf16[1024,512]{1,0:T(8,128)(2,1)} %refs_0_.1, bf16[1024,512]{1,0:T(8,128)(2,1)} %refs_1_.1, f32[8,128,128]{2,1,0:T(8,128)} %bitcast.10, s32[64]{0:T(128)} %copy-done, s32[64]{0:T(128)} %copy-done.1, f32[2,512]{1,0:T(2,128)} %gains.1), custom_call_target="tpu_custom_call" | custom-call | tf_op jit(solution)/shard_map/block/pallas_call | solution.py:783
  148.3 98.6 %update.1 = (f32[8,128,128]{2,1,0:T(8,128)}, f32[8,128,128]{2,1,0:T(8,128)}, f32[8,128,128]{2,1,0:T(8,128)}, bf16[8,128,128]{2,1,0:T(8,128)(2,1)}, f32[2,512]{1,...) custom-call(s32[8]{0:T(128)} %dynamic_slice.3.low, ...), custom_call_target="tpu_custom_call" | custom-call | tf_op jit(solution)/shard_map/update/pallas_call | solution.py:886
Async XLA Ops:
  1.6 0.5 copy-start
  2.2 0.5 copy-start.1

commit v5 on v4

--- a/solution.py
+++ b/solution.py
@@ -101,173 +101,165 @@
 
 
 class Gather:
-    def __init__(self, net, master, rank, slots, weights):
-        self.net, self.slots, self.weights, self.rank = net, slots, weights, rank
+    def __init__(self, net, master, rank, slots, pool, weights, free):
+        self.net, self.weights, self.rank, self.free = net, weights, rank, free
+        self.held = [slots, *pool]
         d, m = lax.axis_index("dp"), lax.axis_index("mp")
         core, col, row = d % 2, (d // 2) % 2, d // 4
         self.me, self.m, self.side = d, m, core
         self.core = d + 1 - 2 * core
         self.plane = [d + 2 - 4 * col, d + 4 - 8 * row, d + 6 - 4 * col - 8 * row]
         self.order = [m, m + 1 - 2 * (m % 2), m + 2 - 4 * (m // 2), 3 - m]
-        self.along, self.spreads = {}, {}
+        self.peers = [(e, m) for e in [self.core] + self.plane] + [(d, k) for k in self.order[1:]]
+        self.along, self.first, self.last, self.inside = {}, {}, {}, {}
         barrier = pltpu.get_barrier_semaphore()
-        for device in [(e, m) for e in [self.core] + self.plane] + [(d, k) for k in self.order[1:]]:
+        for device in self.peers:
             pl.semaphore_signal(barrier, inc=1, device_id=device, device_id_type=MESH)
-        owned = master.shape[0]
-        self.owned = owned
-        for s in range(owned):
-            slots[d * owned + s] = master[s].astype(bf16)
-        pl.semaphore_wait(barrier, 7)
-
-    def rows(self, e, first, count):
-        return self.slots.at[pl.ds(e * self.owned + first, count)]
-
-    def plane_start(self):
-        n, m, (x, y, _) = self.owned, self.m, self.plane
-        h = n // 2
-        self.first = {}
-        for e, first in ((x, 0), (y, h), (x, h), (y, 0)):
-            ref = self.rows(self.me, first, h)
-            self.first[(e is y, first)] = self.net.start(ref, ref, (e, m))
-        ref = self.rows(self.me, 0, n)
-        self.sibling = [self.net.start(ref, ref, (self.core, m))]
-
-    def plane_finish(self):
-        n, m, (x, y, z) = self.owned, self.m, self.plane
-        h = n // 2
-        self.first[(False, 0)].wait_recv()
-        ref = self.rows(x, 0, h)
-        last = [self.net.start(ref, ref, (y, m))]
-        self.first[(True, h)].wait_recv()
-        ref = self.rows(y, h, h)
-        last.append(self.net.start(ref, ref, (x, m)))
-        self.first[(False, h)].wait_recv()
-        ref = self.rows(x, 0, n)
-        self.sibling.append(self.net.start(ref, ref, (self.core, m)))
-        self.first[(True, 0)].wait_recv()
-        ref = self.rows(y, 0, n)
-        self.sibling.append(self.net.start(ref, ref, (self.core, m)))
-        for copy in last:
+        self.n = master.shape[0]
+        for s in range(self.n):
+            slots[d * self.n + s] = master[s].astype(bf16)
+        pl.semaphore_wait(barrier, len(self.peers))
+
+    def rows(self, i, e, first, count):
+        return self.held[i].at[pl.ds(e * self.n + first, count)]
+
+    def along_start(self, i):
+        self.along[i] = self.net.start(
+            self.rows(0, self.me, 0, self.n), self.rows(i, self.me, 0, self.n), (self.me, self.order[i])
+        )
+
+    def send(self, i, e, first, count, to):
+        ref = self.rows(i, e, first, count)
+        return self.net.start(ref, ref, (to, self.m))
+
+    def start(self, i):
+        if i:
+            self.along[i].wait_recv()
+        (x, y, _), h = self.plane, self.n // 2
+        self.first[i] = [self.send(i, self.me, *job) for job in ((0, h, x), (h, h, y), (h, h, x), (0, h, y))]
+        self.inside[i] = [self.send(i, self.me, 0, self.n, self.core)]
+
+    def forward(self, i):
+        (x, y, _), h = self.plane, self.n // 2
+        self.first[i][0].wait_recv()
+        self.last[i] = [self.send(i, x, 0, h, y)]
+        self.first[i][1].wait_recv()
+        self.last[i].append(self.send(i, y, h, h, x))
+
+    def pair(self, i):
+        x, y, z = self.plane
+        self.first[i][2].wait_recv()
+        self.inside[i].append(self.send(i, x, 0, self.n, self.core))
+        self.first[i][3].wait_recv()
+        self.inside[i].append(self.send(i, y, 0, self.n, self.core))
+        for copy in self.last[i]:
             copy.wait_recv()
-        ref = self.rows(z, 0, n)
-        self.sibling.append(self.net.start(ref, ref, (self.core, m)))
-        for copy in self.sibling:
+        self.inside[i].append(self.send(i, z, 0, self.n, self.core))
+
+    def ready(self, i):
+        for copy in self.inside[i]:
             copy.wait_recv()
 
-    def place(self, kinds):
+    def place(self, i):
         wg, wo, wu, wd = self.weights
-        parts, _, hm3 = wg.shape
-        row_tiles, gates = D // BLK, hm3 // BLK
+        row_tiles, gates = D // BLK, wg.shape[2] // BLK
         cols, outs = gates + wu.shape[2] // BLK, wo.shape[1] // BLK
-        for b in range(self.slots.shape[0]):
+        for b in range(row_tiles * cols + (wo.shape[1] + wd.shape[1]) // BLK * row_tiles):
             if b < row_tiles * cols:
                 r, c = b // cols, b % cols
-                kind, ref = (0, wg) if c < gates else (2, wu)
+                ref = wg if c < gates else wu
                 c -= 0 if c < gates else gates
             else:
                 r, c = (b - row_tiles * cols) // row_tiles, (b - row_tiles * cols) % row_tiles
-                kind, ref = (1, wo) if r < outs else (3, wd)
+                ref = wo if r < outs else wd
                 r -= 0 if r < outs else outs
-            if kind in kinds:
-                ref[self.m, r * BLK : (r + 1) * BLK, c * BLK : (c + 1) * BLK] = self.slots[self.rank[b]]
-
-    def share(self, kind, k, e):
-        ref = self.weights[kind]
-        size = ref.shape[1] // 8
-        return ref.at[k, pl.ds(pl.multiple_of(e * size, size), size)]
-
-    def along_start(self, kind, i):
-        ref = self.share(kind, self.m, self.me)
-        self.along[kind, i] = self.net.start(ref, ref, (self.me, self.order[i]))
-
-    def spread(self, kind, i):
-        self.along[kind, i].wait_recv()
-        ref = self.share(kind, self.order[i], self.me)
-        self.spreads[kind, i] = (
-            [self.net.start(ref, ref, (e, self.m)) for e in self.plane],
-            [self.net.start(ref, ref, (self.core, self.m))],
-        )
-
-    def pair(self, kind, i):
-        across, inside = self.spreads[kind, i]
-        for copy, e in zip(across, self.plane):
-            copy.wait_recv()
-            ref = self.share(kind, self.order[i], e)
-            inside.append(self.net.start(ref, ref, (self.core, self.m)))
-
-    def ready(self, kind, i):
-        for copy in self.spreads[kind, i][1]:
-            copy.wait_recv()
+            block = self.held[i][self.rank[b]]
+            ref[self.order[i], r * BLK : (r + 1) * BLK, c * BLK : (c + 1) * BLK] = block
+
+    def done(self):
+        for device in self.peers:
+            pl.semaphore_signal(self.free, inc=1, device_id=device, device_id_type=MESH)
+
+    def all_done(self):
+        pl.semaphore_wait(self.free, len(self.peers))
+
+
+def stack_places(hm, fm):
+    row_tiles, gates, ups, outs = D // BLK, 3 * hm // BLK, fm // BLK, hm // BLK
+    cols = gates + ups
+    first_down = row_tiles * ups
+    first_out = 2 * first_down
+    first_gate = first_out + row_tiles * outs
+    table = []
+    for b in range(row_tiles * (cols + outs + ups)):
+        if b < row_tiles * cols:
+            r, c = b // cols, b % cols
+            table.append(first_gate + r * gates + c if c < gates else r * ups + c - gates)
+        else:
+            k = b - row_tiles * cols
+            table.append(first_out + k if k < row_tiles * outs else first_down + k - row_tiles * outs)
+    return ((0, first_out), (first_out, row_tiles * outs), (first_gate, row_tiles * gates)), table
+
+
+UPDOWN, OUT, GATE = range(3)
 
 
 class Reduce:
-    def __init__(self, net, gather, grads, spans, inside, across, along):
-        self.net, self.g, self.grads, self.spans = net, gather, grads, spans
-        self.inside, self.across, self.along = inside, across, along
-        self.size = grads.shape[1] // 8
+    def __init__(self, net, gather, grads, units, pool):
+        self.net, self.g, self.grads, self.units, self.pool = net, gather, grads, units, pool
+        self.half = grads.shape[1] // 2
+        self.eighth = grads.shape[1] // 8
         self.copies = {}
 
     def place(self, e):
         return (e % 2) * 4 + e // 2
 
-    def rows(self, first, count):
-        return pl.ds(pl.multiple_of(first * self.size, self.size), count * self.size)
-
-    def chip(self, kind, i):
-        g, cols = self.g, self.spans[kind]
-        src = self.grads.at[g.order[i], self.rows((1 - g.side) * 4, 4), cols]
-        dst = self.inside.at[i - 1, :, cols]
-        self.copies[0, kind, i] = self.net.start(src, dst, (g.core, g.m))
-
-    def plane(self, kind, i):
-        g, cols = self.g, self.spans[kind]
-        self.copies[0, kind, i].wait_recv()
+    def chip(self, unit, i):
+        g, (first, count) = self.g, self.units[unit]
+        src = self.grads.at[g.order[i], pl.ds(first + (1 - g.side) * (count // 2), count // 2)]
+        dst = self.pool[i - 1].at[pl.ds(first // 2, count // 2)]
+        self.copies[0, unit, i] = self.net.start(src, dst, (g.core, g.m))
+
+    def plane(self, unit, i):
+        g, (first, count) = self.g, self.units[unit]
+        n = count // 8
+        self.copies[0, unit, i].wait_recv()
         m = g.order[i]
-        rows = self.rows(g.side * 4, 4)
-        total = self.grads[m, rows, cols].astype(f32) + self.inside[i - 1, :, cols].astype(f32)
-        self.grads[m, rows, cols] = total.astype(bf16)
+        rows = pl.ds(first + g.side * (count // 2), count // 2)
+        total = self.grads[m, rows].astype(f32) + self.pool[i - 1][first // 2 : (first + count) // 2].astype(f32)
+        self.grads[m, rows] = total.astype(bf16)
         for k, e in enumerate(g.plane):
-            src = self.grads.at[m, self.rows(self.place(e), 1), cols]
-            self.copies[1, kind, i, k] = self.net.start(src, self.across.at[i - 1, k, :, cols], (e, g.m))
-
-    def model(self, kind, i):
-        g, cols = self.g, self.spans[kind]
+            src = self.grads.at[m, pl.ds(first + self.place(e) * n, n)]
+            dst = self.pool[i - 1].at[pl.ds(self.half + k * self.eighth + first // 8, n)]
+            self.copies[1, unit, i, k] = self.net.start(src, dst, (e, g.m))
+
+    def model(self, unit, i):
+        g, (first, count) = self.g, self.units[unit]
+        n = count // 8
         m = g.order[i]
-        rows = self.rows(self.place(g.me), 1)
-        total = self.grads[m, rows, cols].astype(f32)
+        rows = pl.ds(first + self.place(g.me) * n, n)
+        total = self.grads[m, rows].astype(f32)
         for k in range(3):
-            self.copies[1, kind, i, k].wait_recv()
-            total += self.across[i - 1, k, :, cols].astype(f32)
-        self.grads[m, rows, cols] = total.astype(bf16)
-        src = self.grads.at[m, rows, cols]
-        self.copies[2, kind, i] = self.net.start(src, self.along.at[i - 1, :, cols], (g.me, m))
-
-    def own(self, kind):
-        g, cols = self.g, self.spans[kind]
-        rows = self.rows(self.place(g.me), 1)
-        total = self.grads[g.m, rows, cols].astype(f32)
+            self.copies[1, unit, i, k].wait_recv()
+            total += self.pool[i - 1][pl.ds(self.half + k * self.eighth + first // 8, n)].astype(f32)
+        self.grads[m, rows] = total.astype(bf16)
+        dst = self.pool[i - 1].at[pl.ds(self.half + 3 * self.eighth + first // 8, n)]
+        self.copies[2, unit, i] = self.net.start(self.grads.at[m, rows], dst, (g.me, m))
+
+    def own(self, unit):
+        g, (first, count) = self.g, self.units[unit]
+        n = count // 8
+        rows = pl.ds(first + self.place(g.me) * n, n)
+        total = self.grads[g.m, rows].astype(f32)
         for i in (1, 2, 3):
-            self.copies[2, kind, i].wait_recv()
-            total += self.along[i - 1, :, cols].astype(f32)
-        self.grads[g.m, rows, cols] = total.astype(bf16)
-
-    def into_slots(self, stack, out, slot_order):
-        g = self.g
-        row_tiles = D // BLK
-        gate, outs, ups, downs = self.spans
-        cols = (gate.stop - gate.start + ups.stop - ups.start) // BLK
-        gates, lows = gate.stop // BLK, (outs.stop - outs.start) // BLK
-        for b in range(stack.shape[0]):
-            if b < row_tiles * cols:
-                r, c = b // cols, b % cols
-                first = c * BLK if c < gates else ups.start + (c - gates) * BLK
-            else:
-                k, r = (b - row_tiles * cols) // row_tiles, (b - row_tiles * cols) % row_tiles
-                first = outs.start + k * BLK if k < lows else downs.start + (k - lows) * BLK
-            stack[b] = self.grads[g.m, r * BLK : (r + 1) * BLK, first : first + BLK]
-        n = stack.shape[0] // 8
-        for s in range(stack.shape[0]):
-            out[self.place(s // n) * n + s % n] = stack[slot_order[s]]
+            self.copies[2, unit, i].wait_recv()
+            total += self.pool[i - 1][pl.ds(self.half + 3 * self.eighth + first // 8, n)].astype(f32)
+        self.grads[g.m, rows] = total.astype(bf16)
+
+    def into_slots(self, out, slot_place):
+        n = self.eighth
+        for s in range(8 * n):
+            out[self.place(s // n) * n + s % n] = self.grads[self.g.m, slot_place[s]]
 
     def slots_chip(self, out, pair):
         g, n = self.g, out.shape[0] // 8
@@ -355,9 +347,9 @@
 
 def compute_kernel(linked, *refs):
     if linked:
-        tokens, cotangent, master, rank, slot_order, gains = refs[:6]
+        tokens, cotangent, master, rank, slot_place, gains = refs[:6]
         block_out, input_grad, owned, small = refs[6:10]
-        wg, wo, wu, wd, grads, slots, turned, pair, far, inside, across, along, sum_a, sum_b, sum_c, send, recv = refs[10:27]
+        wg, wo, wu, wd, grads, slots, *pool, pair, far, sum_a, sum_b, sum_c, send, recv, free = refs[10:27]
         scratch = refs[27:]
     else:
         tokens, cotangent, base, wg, wo, wu, wd, gains = refs[:8]
@@ -368,8 +360,7 @@
     parts, _, hm3 = wg.shape
     hm = hm3 // 3
     fm = wu.shape[2]
-    spans = (slice(0, 3 * hm), slice(3 * hm, 4 * hm), slice(4 * hm, 4 * hm + fm), slice(4 * hm + fm, 4 * hm + 2 * fm))
-    gate, outs, ups, downs = spans
+    units, _ = stack_places(hm, fm)
     act, dup, dpre = mid.at[:, :fm], mid.at[:, fm:], mid.at[:, : 3 * hm]
     gain_one = gains[0:1, :]
     gain_two = gains[1:2, :]
@@ -378,6 +369,18 @@
     fetch_tok = pltpu.make_async_copy(tokens, n1, local.at[1])
     fetch_tok.start()
     fetch_cot.start()
+
+    def stack(m, first, value):
+        wide = value.shape[1] // BLK
+        for r in range(value.shape[0] // BLK):
+            for c in range(wide):
+                grads[m, first + r * wide + c] = value[r * BLK : (r + 1) * BLK, c * BLK : (c + 1) * BLK].astype(bf16)
+
+    def stack_turned(m, first, value):
+        high = value.shape[0] // BLK
+        for r in range(high):
+            for c in range(value.shape[1] // BLK):
+                grads[m, first + c * high + r] = value[r * BLK : (r + 1) * BLK, c * BLK : (c + 1) * BLK].astype(bf16)
 
     def permute_in(src, dst):
         for k in range(D // BLK):
@@ -411,9 +414,10 @@
 
     if linked:
         net = Exchange(send, recv)
-        gather = Gather(net, master, rank, slots, (wg, wo, wu, wd))
-        gather.plane_start()
-        reduce = Reduce(net, gather, grads, spans, inside, across, along)
+        gather = Gather(net, master, rank, slots, pool, (wg, wo, wu, wd), free)
+        gather.start(0)
+        gather.along_start(1)
+        reduce = Reduce(net, gather, grads, units, pool)
         order = gather.order
     else:
         order = list(range(parts))
@@ -432,11 +436,15 @@
     n1t[...] = n1[...].T
 
     if linked:
-        gather.plane_finish()
-        gather.place((0,))
-        for i in (1, 2, 3):
-            gather.along_start(0, i)
-        gather.place((1, 2, 3))
+        gather.forward(0)
+        gather.along_start(2)
+        gather.along_start(3)
+    fetch_cot.wait()
+    permute_in(cot, cot)
+    if linked:
+        gather.start(1)
+        gather.pair(0)
+    cott[...] = cot[...].T
 
     fills[0] = jnp.zeros((SUB, hm), f32)
     fills[1] = jnp.ones((SUB, hm), f32)
@@ -444,8 +452,11 @@
     weigh_j = fills[0]
     for turn, m in enumerate(order):
 
-        if linked and turn:
-            gather.ready(0, turn)
+        if linked:
+            if turn:
+                gather.pair(turn)
+            gather.ready(turn)
+            gather.place(turn)
 
         @pl.loop(0, L // R)
         def _(i):
@@ -455,13 +466,10 @@
             admit[m, rows, :] = dot(x, wg[m, :, hm : 2 * hm])
             cand[m, rows, :] = dot(x, wg[m, :, 2 * hm :])
 
-        if linked and turn == 0:
-            gather.spread(0, 1)
-        if linked and turn == 1:
-            gather.pair(0, 2)
-        if linked and turn == 2:
-            for i in (1, 2, 3):
-                gather.pair(1, i)
+        if linked and turn < 3:
+            gather.forward(turn + 1)
+            if turn < 2:
+                gather.start(turn + 2)
 
         def step(j, carry):
             s, p, k_sum, kj_sum = carry
@@ -489,45 +497,14 @@
         for _ in range(SUB - 1):
             enter = shift_down(s + p * enter)
 
-        if linked:
-            if turn == 0:
-                gather.spread(0, 2)
-            if turn == 1:
-                gather.pair(0, 3)
-                for i in (1, 2, 3):
-                    gather.spread(1, i)
-            if turn == 2:
-                gather.spread(2, 1)
-                gather.spread(3, 1)
-            if turn == 3:
-                gather.pair(2, 1)
-                gather.pair(3, 1)
-                gather.spread(2, 2)
-                gather.spread(3, 2)
-            if turn:
-                gather.along_start(2, turn)
-                gather.along_start(3, turn)
-
         @pl.loop(0, J, unroll=4)
         def _(j):
             rows = pl.ds(pl.multiple_of(j * SUB, SUB), SUB)
             state[m, rows, :] = take(0, rows) + take(half, rows) * enter
 
-        if turn == 0:
-            fetch_cot.wait()
-            permute_in(cot, cot)
-            if linked:
-                gather.pair(0, 1)
-                gather.spread(0, 3)
-                for i in (1, 2, 3):
-                    gather.along_start(1, i)
-            cott[...] = cot[...].T
-
-    if linked:
-        for i in (1, 2, 3):
-            gather.ready(1, i)
-        for kind in (2, 3):
-            gather.spread(kind, 3)
+    if linked:
+        net.drain()
+        gather.done()
 
     @pl.loop(0, L // R)
     def _(i):
@@ -544,10 +521,6 @@
     n2t[...] = n2[...].T
 
     for turn, m in enumerate(order):
-
-        if linked and turn:
-            gather.ready(2, turn)
-            gather.ready(3, turn)
 
         @pl.loop(0, L // R)
         def _(i):
@@ -562,30 +535,24 @@
             acc_a[rows, :] += dot(ac, wd[m])
             acc_b[rows, :] += dot(du, wu[m], True)
 
-        if linked and turn < 2:
-            gather.pair(2, turn + 2)
-            gather.pair(3, turn + 2)
         if linked and turn >= 2:
-            reduce.plane(2, turn - 1)
-            reduce.plane(3, turn - 1)
+            reduce.plane(UPDOWN, turn - 1)
         if linked and turn == 3:
-            reduce.model(2, 1)
-            reduce.model(3, 1)
-            net.drain()
-        grads[m, :, downs] = dot(cott[...], act[...]).astype(bf16)
-        grads[m, :, ups] = dot(n2t[...], dup[...]).astype(bf16)
+            reduce.model(UPDOWN, 1)
+        stack(m, 0, dot(n2t[...], dup[...]))
+        stack_turned(m, units[UPDOWN][1] // 2, dot(cott[...], act[...]))
         if linked and turn:
-            reduce.chip(2, turn)
-            reduce.chip(3, turn)
+            if turn == 1:
+                gather.all_done()
+            reduce.chip(UPDOWN, turn)
 
     permute_out(acc_a, n1)
     push_out = pltpu.make_async_copy(n1, block_out, local.at[0])
     push_out.start()
 
     if linked:
-        for kind in (2, 3):
-            reduce.plane(kind, 3)
-            reduce.model(kind, 2)
+        reduce.plane(UPDOWN, 3)
+        reduce.model(UPDOWN, 2)
 
     gain_sum_two = jnp.zeros((1, D), f32)
 
@@ -607,9 +574,9 @@
     fetch_tok.start()
 
     for turn, m in reversed(list(enumerate(order))):
-        grads[m, :, outs] = dot(dmlt[...], state[m].astype(bf16)).astype(bf16)
+        stack_turned(m, units[OUT][0], dot(dmlt[...], state[m].astype(bf16)))
         if linked and turn:
-            reduce.chip(1, turn)
+            reduce.chip(OUT, turn)
 
     for turn, m in reversed(list(enumerate(order))):
 
@@ -642,20 +609,19 @@
 
         if linked:
             if turn == 3:
-                for kind in (2, 3):
-                    reduce.model(kind, 3)
+                reduce.model(UPDOWN, 3)
                 for i in (3, 2, 1):
-                    reduce.plane(1, i)
+                    reduce.plane(OUT, i)
             if turn < 3:
-                reduce.plane(0, turn + 1)
+                reduce.plane(GATE, turn + 1)
             if turn == 2:
                 for i in (3, 2, 1):
-                    reduce.model(1, i)
+                    reduce.model(OUT, i)
             if turn < 2:
-                reduce.model(0, turn + 2)
+                reduce.model(GATE, turn + 2)
             if turn == 0:
-                for kind in (1, 2, 3):
-                    reduce.own(kind)
+                reduce.own(OUT)
+                reduce.own(UPDOWN)
 
         def back(i, before):
             parts_out = []
@@ -679,9 +645,9 @@
         last = state[m, pl.ds(L - SUB, SUB), :]
         lax.fori_loop(0, J // 2, back, shift_down(last), unroll=2)
 
-        grads[m, :, gate] = dot(n1t[...], dpre[...]).astype(bf16)
+        stack(m, units[GATE][0], dot(n1t[...], dpre[...]))
         if linked and turn:
-            reduce.chip(0, turn)
+            reduce.chip(GATE, turn)
 
         @pl.loop(0, L // R)
         def _(i):
@@ -692,7 +658,7 @@
     permute_in(cot, cot)
 
     if linked:
-        reduce.model(0, 1)
+        reduce.model(GATE, 1)
 
     def back_one(i, total):
         rows = pl.ds(pl.multiple_of(i * R, R), R)
@@ -721,12 +687,12 @@
     if linked:
         tiny = SmallSum(net, gather, small, sum_a, sum_b, sum_c)
         tiny.send(0)
-        reduce.own(0)
-        reduce.into_slots(slots, turned, slot_order)
-        reduce.slots_chip(turned, pair)
+        reduce.own(GATE)
+        reduce.into_slots(slots, slot_place)
+        reduce.slots_chip(slots, pair)
         tiny.add(0)
         tiny.send(1)
-        reduce.slots_plane(turned, pair, far)
+        reduce.slots_plane(slots, pair, far)
 
     permute_out(mixed, acc_a)
     push_grad = pltpu.make_async_copy(acc_a, input_grad, local.at[2])
@@ -735,23 +701,23 @@
     if linked:
         tiny.add(1)
         tiny.send(2)
-        reduce.slots_end(turned, pair, far, owned)
+        reduce.slots_end(slots, pair, far, owned)
         tiny.add(2)
         net.drain()
     push_out.wait()
     push_grad.wait()
 
 
-def compute(tokens, cotangent, gains, weights=None, base=None, master=None, rank=None, slot_order=None):
+def compute(tokens, cotangent, gains, weights=None, base=None, master=None, rank=None, slot_place=None):
     linked = weights is None
     parts = lax.axis_size("mp")
     hm, fm = H // parts, FF // parts
-    wide = 4 * hm + 2 * fm
+    stacked = (parts, D * (4 * hm + 2 * fm) // BLK**2, BLK, BLK)
     sds = jax.ShapeDtypeStruct
     vm, sm, hbm = (pl.BlockSpec(memory_space=k) for k in (pltpu.VMEM, pltpu.SMEM, pl.ANY))
     if linked:
         n = rank.shape[0]
-        args = (tokens, cotangent, master, rank, slot_order, gains)
+        args = (tokens, cotangent, master, rank, slot_place, gains)
         in_specs = [hbm, hbm, vm, sm, sm, vm]
         middle = sds((n // 8, BLK, BLK), f32)
         extra = [
@@ -759,25 +725,23 @@
             pltpu.VMEM((parts, hm, D), bf16),
             pltpu.VMEM((parts, D, fm), bf16),
             pltpu.VMEM((parts, fm, D), bf16),
-            pltpu.VMEM((parts, D, wide), bf16),
+            pltpu.VMEM(stacked, bf16),
             pltpu.VMEM((n, BLK, BLK), bf16),
-            pltpu.VMEM((n, BLK, BLK), bf16),
+            *[pltpu.VMEM((n, BLK, BLK), bf16) for _ in range(parts - 1)],
             pltpu.VMEM((n // 2, BLK, BLK), bf16),
             pltpu.VMEM((6, n // 16, BLK, BLK), bf16),
-            pltpu.VMEM((3, D // 2, wide), bf16),
-            pltpu.VMEM((3, 3, D // 8, wide), bf16),
-            pltpu.VMEM((3, D // 8, wide), bf16),
             pltpu.VMEM((parts, 8, D), f32),
             pltpu.VMEM((4, 8, D), f32),
             pltpu.VMEM((2, 8, D), f32),
-            pltpu.SemaphoreType.DMA((256,)),
-            pltpu.SemaphoreType.DMA((256,)),
+            pltpu.SemaphoreType.DMA((128,)),
+            pltpu.SemaphoreType.DMA((128,)),
+            pltpu.SemaphoreType.REGULAR,
         ]
         params = dict(collective_id=0, has_side_effects=True)
     else:
         args = (tokens, cotangent, base, *weights, gains)
         in_specs = [hbm, hbm, sm] + [vm] * 5
-        middle = sds((parts, D, wide), bf16)
+        middle = sds(stacked, bf16)
         extra = []
         params = {}
     return pl.pallas_call(
@@ -834,9 +798,11 @@
     given, refs = refs[:passed], refs[passed:]
     first_new, second_new, master_new, master_low, gain_first, gain_second, gains_new, forget_mean = refs[:8]
     copied, refs = refs[8 : 8 + passed], refs[8 + passed :]
-    held, made, made_low, sem_in, sem_out, sem_pass = refs
+    held, made, made_low, sem_in, sem_out, sem_pass = refs[:6]
+    passage = refs[6:]
     count = master.shape[0]
-    passing = [pltpu.make_async_copy(src, dst, sem_pass.at[k]) for k, (src, dst) in enumerate(zip(given, copied))]
+    enter = [pltpu.make_async_copy(src, via, sem_pass.at[0, k]) for k, (src, via) in enumerate(zip(given, passage))]
+    leave = [pltpu.make_async_copy(via, dst, sem_pass.at[1, k]) for k, (via, dst) in enumerate(zip(passage, copied))]
     sources = (owned, basis_left, basis_right, moment_one, moment_two, master)
     fetch = [
         [pltpu.make_async_copy(src.at[s], held.at[s, k], sem_in.at[s, k]) for k, src in enumerate(sources)]
@@ -845,12 +811,16 @@
     for row in fetch:
         for copy in row:
             copy.start()
-    for copy in passing:
+    for copy in enter:
         copy.start()
     push = []
     for s in range(count):
         for copy in fetch[s]:
             copy.wait()
+        if s == min(2, count - 1):
+            for come, go in zip(enter, leave):
+                come.wait()
+                go.start()
         grad = held[s, 0]
         grad = jnp.where(low[s] >= low_first, grad.T, grad)
         left, right = held[s, 1], held[s, 2]
@@ -874,7 +844,7 @@
     gain_second[...] = second
     gains_new[...] = gains[...] - gain_rate * direction
     forget_mean[...] = jnp.sum(sums[2:3, :], axis=1, keepdims=True) * (1.0 / (H * (token_total + 1) / 2.0))
-    for copy in push + passing:
+    for copy in push + leave:
         copy.wait()
 
 
@@ -898,8 +868,9 @@
             pltpu.VMEM((count, BLK, BLK), bf16),
             pltpu.SemaphoreType.DMA((count, 6)),
             pltpu.SemaphoreType.DMA((count, 4)),
-            pltpu.SemaphoreType.DMA((max(len(passed), 1),)),
-        ],
+            pltpu.SemaphoreType.DMA((2, len(passed))),
+        ]
+        + [pltpu.VMEM(v.shape, v.dtype) for v in passed],
         compiler_params=pltpu.CompilerParams(vmem_limit_bytes=56 * 2**20),
         name="update",
     )(*small, *large, *passed)
@@ -928,9 +899,12 @@
     ahead = (owner[None, :] < owner[:, None]) | ((owner[None, :] == owner[:, None]) & (number[None, :] < number[:, None]))
     block_rank = jnp.sum(ahead.astype(jnp.int32), axis=1)
     slot_order = jnp.sum(jnp.where(block_rank[None, :] == number[:, None], number[None, :], 0), axis=1)
+    _, table = stack_places(hm, fm)
+    table = jnp.asarray(table, jnp.int32)
+    slot_place = jnp.sum(jnp.where(block_rank[None, :] == number[:, None], table[None, :], 0), axis=1)
     if data_parts == 8 and parts == 4:
         block_out, input_grad, owned, sums = compute(
-            tokens, cotangent, gains, master=master[0], rank=block_rank, slot_order=slot_order
+            tokens, cotangent, gains, master=master[0], rank=block_rank, slot_place=slot_place
         )
     else:
         stored = lax.all_gather(master.astype(bf16), "dp", axis=1, tiled=True)
@@ -944,14 +918,7 @@
         first = ((lax.axis_index("dp") * parts + lax.axis_index("mp")) * L + 1).astype(f32)
         base = jnp.stack([first, jnp.asarray(token_total, f32)])
         block_out, input_grad, grads, sums = compute(tokens, cotangent, gains, weights=weights, base=base)
-        upper = jnp.concatenate([grads[:, :, : 3 * hm], grads[:, :, 4 * hm : 4 * hm + fm]], axis=2)
-        upper = upper.reshape(parts, row_tiles, BLK, cols, BLK).transpose(0, 1, 3, 2, 4)
-        lower = jnp.concatenate([grads[:, :, 3 * hm : 4 * hm], grads[:, :, 4 * hm + fm :]], axis=2)
-        lower = lower.reshape(parts, row_tiles, BLK, lows, BLK).transpose(0, 3, 1, 2, 4)
-        natural = jnp.concatenate(
-            [upper.reshape(parts, -1, BLK, BLK), lower.reshape(parts, -1, BLK, BLK)], axis=1
-        ).astype(f32)
-        owned = lax.psum_scatter(natural[:, slot_order], "dp", scatter_dimension=1, tiled=True)
+        owned = lax.psum_scatter(grads[:, slot_place].astype(f32), "dp", scatter_dimension=1, tiled=True)
         owned = lax.psum_scatter(owned, "mp", scatter_dimension=0, tiled=True)[0]
         sums = lax.psum(sums, ("dp", "mp"))
     mine = lax.dynamic_slice_in_dim(slot_order, lax.axis_index("dp") * master.shape[1], master.shape[1])

time: 247 us -> 153 us (0.62)
  Pallas kernels: 244 us -> 149 us
    pallas_call x1, Pallas kernels: 98.6 us -> 11 us  [update(): pl.pallas_call(functools.partial(update_kernel, low_first, token_total, l...]
    pallas_call x1, Pallas kernels: 145 us -> 138 us  [compute(): pl.pallas_call(functools.partial(compute_kernel, linked), out_shape=(sds(...]
where the time goes in v5:
time: 153 us
  Pallas kernels  149 us (97%)
  other arithmetic  2.19 us (1%)
    pallas_call x1, Pallas kernels, compute(): pl.pallas_call(functools.partial(compute_kernel, linked), out_shape=(sds(...  138 us
    pallas_call x1, Pallas kernels, update(): pl.pallas_call(functools.partial(update_kernel, low_first, token_total, l...  11 us

profile of v5, /device:TPU:0, one launch (start us, length us, event | category | flops | bytes accessed | tf_op | source)
XLA Modules:
  0.0 152.7 jit_solution(1188513567503789092)
XLA Ops:
  0.6 0.9 convert_reduce_fusion.refs_3_
  1.6 0.0 copy-start
  1.6 0.5 copy-done
  2.1 1.3 select_reduce_fusion
  3.4 0.7 dynamic_slice.3.low
  4.0 137.5 %block.1 = (bf16[1024,512]{1,0:T(8,128)(2,1)}, f32[1024,512]{1,0:T(8,128)}, f32[8,128,128]{2,1,0:T(8,128)}, f32[8,512]{1,0:T(8,128)}) custom-call(bf16[1024,512]{1,0:T(8,128)(2,1)} %refs_0_.1, bf16[1024,512]{1,0:T(8,128)(2,1)} %refs_1_.1, f32[8,128,128]{2,1,0:T(8,128)} %bitcast.10, s32[64]{0:T(128)} %copy-done, s32[64]{0:T(128)} %get-tuple-element.38.refs_4_, ...), custom_call_target="tpu_custom_call" | custom-call | tf_op jit(solution)/shard_map/block/pallas_call | solution.py:747
  141.6 11.0 %update.1 = (f32[8,128,128]{2,1,0:T(8,128)}, f32[8,128,128]{2,1,0:T(8,128)}, f32[8,128,128]{2,1,0:T(8,128)}, bf16[8,128,128]{2,1,0:T(8,128)(2,1)}, f32[2,512]{1,...) custom-call(s32[8]{0:T(128)} %dynamic_slice.3.low, ...), custom_call_target="tpu_custom_call" | custom-call | tf_op jit(solution)/shard_map/update/pallas_call | solution.py:856
Async XLA Ops:
  1.6 0.5 copy-start
